TPU v7x, 512 devices: a whole 4x8x8 slice. The times are simulated.
512 devices in a mesh: ctx: 64 (over x, z, core), vocab: 8 (over y).
Axes of the slice: x: 4, y: 8, z: 8, core: 2. Of those that a mesh axis runs over, the one named last changes fastest.
Arguments:
- hidden: bfloat16 [16384, 8192], P('ctx', 'vocab'), may hold values from -540 to 540
- norm_gain: float32 [8192], P('vocab'), may hold values from 0.5 to 1.5
- head: bfloat16 [63232, 8192], P('ctx', 'vocab'), may hold values from -0.53033009 to 0.53033009
- masked_pos: int32 [2, 64], replicated, may hold values from 0 to 8191, as said below
- masked_targets: int32 [2, 64], replicated, may hold values from 0 to 63231
- t_num: int32 [2], replicated, may hold values from 1 to 3, as said below
- t_den: int32 [2], replicated, may hold values from 192 to 319
Outputs:
- loss_value: float32 [], replicated
- grad_hidden: bfloat16 [16384, 8192], P('ctx', 'vocab')
- grad_head: bfloat16 [63232, 8192], P('ctx', 'vocab')
- grad_gain: float32 [8192], P('vocab')
Inputs may be any that keep to these rules, and one draw needn't show every extreme that they name: `masked_pos`: each row lists 64 distinct positions of one sequence in increasing order; at most 8 of them fall in one aligned block of 256 positions, and exactly 8 in some blocks of every sequence. `t_num`: the two numerators differ.
All inputs are finite; a program needn't handle non-finite values.
Results may differ from a plain program's by a relative error of at most 0.0081.
Values may be sent and summed in bfloat16 or wider, within the bound.
A program may use at most 64 MiB of HBM per device.

v0:
```python
import jax
import jax.numpy as jnp
from jax import lax
from jax.sharding import PartitionSpec as P

CAP = 8


EPSILON = 1e-05
LOSS_SCALE = 1024.0


def contract_last(left, right):
    return lax.dot_general(
        left, right, (((1,), (1,)), ((), ())), preferred_element_type=jnp.float32
    )


def on_device(hidden, norm_gain, head, masked_pos, masked_targets, t_num, t_den):
    tok_here, width_here = hidden.shape
    voc_here = head.shape[0]
    ctx_count = lax.axis_size("ctx")
    vocab_count = lax.axis_size("vocab")
    ctx_index = lax.axis_index("ctx")
    vocab_index = lax.axis_index("vocab")
    blocks = ctx_count // 2
    slot_count = masked_pos.shape[1]
    model_width = width_here * vocab_count
    seq_here = ctx_index // blocks
    block_here = ctx_index % blocks
    block_of = masked_pos // tok_here
    block_ids = jnp.arange(blocks, dtype=jnp.int32)
    counts = jnp.sum((block_of[:, :, None] == block_ids[None, None, :]).astype(jnp.int32), axis=1)
    offsets = jnp.cumsum(counts, axis=1) - counts
    weight = t_den.astype(jnp.float32) / (t_num.astype(jnp.float32) * (2.0 * tok_here * blocks))
    lane_ids = jnp.arange(CAP, dtype=jnp.int32)
    own_count = counts[seq_here, block_here]
    own_start = offsets[seq_here, block_here]
    own_valid = lane_ids < own_count
    seq_list = jnp.concatenate([masked_pos[seq_here], jnp.zeros((CAP,), jnp.int32)])
    own_pos = lax.dynamic_slice_in_dim(seq_list, own_start, CAP) - block_here * tok_here
    own_pos = jnp.where(own_valid, own_pos, 0)
    own_rows = jnp.where(own_valid[:, None], hidden[own_pos].astype(jnp.float32), 0.0)
    squares = lax.psum(jnp.sum(own_rows * own_rows, axis=1), "vocab")
    inverse = lax.rsqrt(squares / model_width + EPSILON)
    normed_own = (own_rows * inverse[:, None] * norm_gain[None, :]).astype(jnp.bfloat16)
    normed_all = lax.all_gather(normed_own, "ctx", axis=0, tiled=True)
    row_ids = jnp.arange(ctx_count * CAP, dtype=jnp.int32)
    owner_ctx = row_ids // CAP
    lane_of = row_ids % CAP
    owner_seq = owner_ctx // blocks
    owner_block = owner_ctx % blocks
    row_valid = lane_of < counts[owner_seq, owner_block]
    list_slot = jnp.minimum(offsets[owner_seq, owner_block] + lane_of, slot_count - 1)
    row_targets = masked_targets[owner_seq, list_slot]
    row_factor = jnp.where(row_valid, weight[owner_seq], 0.0)
    row_total = normed_all.shape[0]
    rows_block = row_total // vocab_count
    logits = lax.psum_scatter(
        contract_last(normed_all, head), "vocab", scatter_dimension=0, tiled=True
    )
    block_start = vocab_index * rows_block
    target_cols = (
        lax.dynamic_slice_in_dim(row_targets, block_start, rows_block) - ctx_index * voc_here
    )
    factor = lax.dynamic_slice_in_dim(row_factor, block_start, rows_block)
    columns = jnp.arange(voc_here, dtype=jnp.int32)
    is_target = columns[None, :] == target_cols[:, None]
    picked = jnp.sum(jnp.where(is_target, logits, 0.0), axis=1)
    local_top = jnp.max(logits, axis=1)
    row_top = lax.pmax(local_top, "ctx")
    exp_total, picked = lax.psum(
        (jnp.sum(jnp.exp(logits - row_top[:, None]), axis=1), picked), "ctx"
    )
    log_total = row_top + jnp.log(exp_total)
    loss_value = lax.psum(jnp.sum(factor * (log_total - picked)), "vocab")
    softmax_out = jnp.exp(logits - log_total[:, None])
    dlogits = (
        (LOSS_SCALE * factor)[:, None] * (softmax_out - is_target.astype(jnp.float32))
    ).astype(jnp.bfloat16)
    all_grads = lax.all_gather(dlogits, "vocab", axis=0, tiled=True)
    grad_head = lax.dot_general(
        all_grads, normed_all, (((0,), (0,)), ((), ())), preferred_element_type=jnp.float32
    ).astype(jnp.bfloat16)
    own_grad = lax.psum_scatter(
        jnp.dot(all_grads, head, preferred_element_type=jnp.float32),
        "ctx",
        scatter_dimension=0,
        tiled=True,
    )
    own_grad = jnp.where(own_valid[:, None], own_grad, 0.0)
    grad_gain = lax.psum(jnp.sum(own_grad * own_rows * inverse[:, None], axis=0), "ctx")
    inner_mean = (
        lax.psum(jnp.sum(norm_gain[None, :] * own_grad * own_rows, axis=1), "vocab") / model_width
    )
    row_grads = (
        inverse[:, None] * norm_gain[None, :] * own_grad
        - own_rows * (inverse * inverse * inverse * inner_mean)[:, None]
    )
    write_rows = jnp.where(own_valid, own_pos, tok_here)
    grad_hidden = (
        jnp.zeros((tok_here, width_here), jnp.bfloat16)
        .at[write_rows]
        .set(row_grads.astype(jnp.bfloat16), mode="drop")
    )
    return (loss_value, grad_hidden, grad_head, grad_gain)


def solution(mesh):
    placed = (P("ctx", "vocab"), P("vocab"), P("ctx", "vocab"), P(), P(), P(), P())
    return jax.shard_map(
        on_device,
        mesh=mesh,
        in_specs=placed,
        out_specs=(P(), P("ctx", "vocab"), P("ctx", "vocab"), P("vocab")),
        check_vma=False,
    )
```

profile of v0, /device:TPU:1, one launch (start us, length us, event | category | flops | bytes accessed | tf_op | source)
XLA Modules:
  0.0 739.9 jit_solution(13725821811192345752)
XLA Ops:
  7.2 0.0 copy-start
  7.2 0.0 all-gather.2.cloned.1.call-start
  7.3 0.8 and_select_fusion.4
  8.1 0.1 convert_reduce_fusion
  8.2 0.2 reduce_window_sum.11
  8.4 0.7 dynamic-slice_bitcast_fusion
  9.1 0.6 dynamic_slice.19
  9.7 0.6 dynamic_slice.21
  11.6 0.7 iota_compare_fusion.2
  12.9 0.7 compare_select_fusion.7
  13.6 1.7 gather_fusion.1
  15.3 0.2 multiply_reduce_fusion.2
  15.5 14.7 %psum.42 = f32[8]{0:T(128)S(1)} all-reduce(f32[8]{0:T(128)S(1)} %multiply_reduce_fusion.2), channel_id=1, replica_groups=mesh['ctx'=64,'vocab'=8] {'vocab'}, use_global_device_ids=true, to_apply=%region_3.4 | all-reduce | flops 8 | bytes 64 | tf_op jit(solution)/shard_map/psum | solution.py:44
  30.2 1.4 multiply_convert_fusion.1
  31.6 0.0 all-gather.2.cloned.1.call-update
  31.6 0.0 reduce-scatter.3.cloned.1.call-start
  31.6 88.7 %all-gather.2.cloned.1.call-done = bf16[512,1024]{1,0:T(8,128)(2,1)} async-done(((bf16[8,1024]{1,0:T(8,128)(2,1)}), bf16[512,1024]{1,0:T(8,128)(2,1)}) %all-gather.2.cloned.1.call-update) | async-done | bytes 1048592 | tf_op jit(solution)/shard_map/all_gather | solution.py:47
  120.3 0.0 copy-done
  120.3 3.9 fusion.22
  124.2 0.0 reduce-scatter.3.cloned.1.call-update
  124.2 0.0 reduce-scatter.5.cloned.1.call-start
  124.3 0.0 copy-start.1
  124.3 4.8 gather_fusion.2
  129.0 0.0 copy-start.3
  129.0 0.0 copy-start.4
  129.1 4.8 gather_fusion
  133.9 4.8 gather_fusion.3
  138.7 0.6 fusion.21
  139.2 1.3 compare_select_fusion.3
  140.6 0.1 broadcast_multiply_fusion
  140.6 0.1 dynamic-slice_subtract_fusion
  140.7 20.8 %reduce-scatter.3.cloned.1.call-done = f32[64,988]{1,0:T(8,128)} async-done(((f32[512,988]{1,0:T(8,128)}), f32[64,988]{1,0:T(8,128)}) %reduce-scatter.3.cloned.1.call-update) | async-done | bytes 252944 | tf_op jit(solution)/shard_map/reduce_scatter | solution.py:59
  161.5 1.1 reduce_max.9
  162.6 129.0 %pmax.7 = f32[64]{0:T(128)S(1)} all-reduce(f32[64]{0:T(128)S(1)} %reduce_max.9), channel_id=1, replica_groups=mesh['ctx'=64,'vocab'=8] {'ctx'}, use_global_device_ids=true, to_apply=%region_6.7 | all-reduce | flops 64 | bytes 512 | tf_op jit(solution)/shard_map/pmax | solution.py:71
  291.6 1.2 select_reduce_fusion
  292.8 124.8 %psum.43 = f32[64]{0:T(128)S(1)} all-reduce(f32[64]{0:T(128)S(1)} %get-tuple-element.5), channel_id=1, replica_groups=mesh['ctx'=64,'vocab'=8] {'ctx'}, use_global_device_ids=true, to_apply=%region_8.9 | all-reduce | flops 64 | bytes 512 | tf_op jit(solution)/shard_map/psum | solution.py:72
  417.6 1.1 multiply_convert_fusion
  418.7 21.1 %all_gather.7 = bf16[512,988]{1,0:T(8,128)(2,1)S(1)} all-gather(bf16[64,988]{1,0:T(8,128)(2,1)S(1)} %multiply_convert_fusion), channel_id=1, replica_groups=mesh['ctx'=64,'vocab'=8] {'vocab'}, dimensions={0}, use_global_device_ids=true | all-gather | bytes 1138176 | tf_op jit(solution)/shard_map/all_gather | solution.py:81
  439.9 2.6 fusion.23
  442.5 0.0 reduce-scatter.5.cloned.1.call-update
  442.5 0.0 copy-start.2
  442.5 3.8 convolution_convert_fusion
  446.3 138.0 %reduce-scatter.5.cloned.1.call-done = f32[8,1024]{1,0:T(8,128)} async-done(((f32[512,1024]{1,0:T(8,128)}), f32[8,1024]{1,0:T(8,128)}) %reduce-scatter.5.cloned.1.call-update) | async-done | bytes 32784 | tf_op jit(solution)/shard_map/reduce_scatter | solution.py:85
  584.3 1.0 multiply_reduce_fusion
  585.3 131.7 %all-reduce.1 = (f32[64]{0:T(128)S(1)}, f32[1024]{0:T(1024)}) all-reduce(f32[64]{0:T(128)S(1)} %get-tuple-element.4, f32[1024]{0:T(1024)S(1)} %get-tuple-element.6), channel_id=1, replica_groups=mesh['ctx'=64,'vocab'=8] {'ctx'}, use_global_device_ids=true, to_apply=%region_10.11 | all-reduce | flops 1088 | bytes 8704 | tf_op jit(solution)/shard_map/psum | solution.py:72
  717.0 0.7 multiply_reduce_fusion.3
  717.7 13.9 %all-reduce.2 = (f32[]{:T(128)}, f32[8]{0:T(128)S(1)}) all-reduce(f32[]{:T(128)} %multiply_reduce_fusion.3, f32[8]{0:T(128)S(1)} %get-tuple-element.7), channel_id=1, replica_groups=mesh['ctx'=64,'vocab'=8] {'vocab'}, use_global_device_ids=true, to_apply=%region_12.13 | all-reduce | flops 9 | bytes 72 | tf_op jit(solution)/shard_map/psum | solution.py:76
  731.6 1.8 scatter_custom_fusion
  (14 shorter events, 0.1 us)
Async XLA Ops:
  7.2 113.1 %copy-start = (bf16[988,1024]{1,0:T(8,128)(2,1)S(1)}, bf16[988,1024]{1,0:T(8,128)(2,1)}, u32[]{:S(2)}) copy-start(bf16[988,1024]{1,0:T(8,128)(2,1)} %param.9) | copy-start | bytes 6070276
  7.2 113.1 %all-gather.2.cloned.1.call-start = ((), (), s32[]{:S(2)}) async-start(), calls=%async_computation.2 | async-start | bytes 1064960 | tf_op jit(solution)/shard_map/all_gather | solution.py:47
  31.6 129.9 %reduce-scatter.3.cloned.1.call-start = ((), (), s32[]{:S(2)}) async-start(), calls=%async_computation.3 | async-start | bytes 2359296 | tf_op jit(solution)/shard_map/reduce_scatter | solution.py:59
  124.2 460.1 %reduce-scatter.5.cloned.1.call-start = ((), (), s32[]{:S(2)}) async-start(), calls=%async_computation.4 | async-start | bytes 2129920 | tf_op jit(solution)/shard_map/reduce_scatter | solution.py:85
  124.3 9.6 %copy-start.1 = (s32[2,64]{1,0:T(2,128)S(1)}, s32[2,64]{1,0:T(2,128)}, u32[]{:S(2)}) copy-start(s32[2,64]{1,0:T(2,128)} %param.11) | copy-start | bytes 1540
  129.0 9.6 %copy-start.3 = (s32[2]{0:T(128)S(1)}, s32[2]{0:T(128)}, u32[]{:S(2)}) copy-start(s32[2]{0:T(128)} %param.12) | copy-start | bytes 28
  129.0 9.6 %copy-start.4 = (s32[2]{0:T(128)S(1)}, s32[2]{0:T(128)}, u32[]{:S(2)}) copy-start(s32[2]{0:T(128)} %param.13) | copy-start | bytes 28
  442.5 141.8 %copy-start.2 = (f32[1024]{0:T(1024)S(1)}, f32[1024]{0:T(1024)}, u32[]{:S(2)}) copy-start(f32[1024]{0:T(1024)} %param.8) | copy-start | bytes 12292
Sparse Core Ops, SparseCore 0:
  31.7 88.5 all-gather.1
  124.3 37.1 reduce-scatter.2
  442.6 141.6 reduce-scatter.4
where the time goes:
time: 742 us; the launch traced here: 740 us
  blocking collectives  435 us (59%)
  waiting for transfers between devices  247 us (33%)
  local copies, waits for them, and re-layouts  18.4 us (2%)
  between operations  15.9 us (2%)
  other arithmetic  12.5 us (2%)
  matrix products  10.3 us (1%)
    psum x2, blocking collectives, on_device(): lax.psum((jnp.sum(jnp.exp(logits - row_top[:, None]), axis=1), picked), '...  257 us
    reduce_scatter x1, waiting for transfers between devices, on_device(): lax.psum_scatter(jnp.dot(all_grads, head, preferred_element_type=jnp.floa...  138 us
    pmax x1, blocking collectives, on_device(): row_top = lax.pmax(local_top, 'ctx')  129 us
    all_gather x1, waiting for transfers between devices, on_device(): normed_all = lax.all_gather(normed_own, 'ctx', axis=0, tiled=True)  88.7 us
    all_gather x1, blocking collectives, on_device(): all_grads = lax.all_gather(dlogits, 'vocab', axis=0, tiled=True)  21.1 us
    reduce_scatter x1, waiting for transfers between devices, on_device(): lax.psum_scatter(contract_last(normed_all, head), 'vocab', scatter_dimens...  20.8 us
  transfers between devices with their start and end apart: 3, of which 3 were waited for; matrix products, arithmetic and copies ran while one was open for 3% of the time, Pallas kernels for 0%

commit v1 on v0

v1 whole, which is shorter than its diff:
```python
import jax
import jax.numpy as jnp
from jax import lax
from jax.experimental import pallas as pl
from jax.experimental.pallas import tpu as pltpu
from jax.sharding import PartitionSpec as P

MESH = pl.DeviceIdType.MESH
F32 = jnp.float32
BF16 = jnp.bfloat16
EPSILON = 1e-05
LOSS_SCALE = 1024.0
NX, NZ, NY = 4, 8, 8
ROWS = 128
SEQ_ROWS = 64
TOK = 256
WIDTH = 1024
MODEL = 8192
PADDED = 1024


def iota(shape, dim):
    return lax.broadcasted_iota(jnp.int32, shape, dim)


def column_of(lanes):
    n = lanes.shape[1]
    same = iota((n, n), 0) == iota((n, n), 1)
    return jnp.sum(jnp.where(same, lanes, 0.0), axis=1, keepdims=True)


def lanes_of(column):
    n = column.shape[0]
    same = iota((n, n), 0) == iota((n, n), 1)
    return jnp.sum(jnp.where(same, column, 0.0), axis=0, keepdims=True)


def combine(tiles):
    top = tiles[0][0:1]
    for t in tiles[1:]:
        top = jnp.maximum(top, t[0:1])
    total = weighted = picked = None
    for t in tiles:
        shift = t[0:1] - top
        scale = jnp.exp(shift)
        a = scale * t[1:2]
        b = scale * (t[2:3] + shift * t[1:2])
        c = t[3:4]
        total = a if total is None else total + a
        weighted = b if weighted is None else weighted + b
        picked = c if picked is None else picked + c
    return stack_rows(top, total, weighted, picked)


def stack_rows(*rows):
    sub = iota((8, ROWS), 0)
    out = jnp.zeros((8, ROWS), F32)
    for i, r in enumerate(rows):
        out = jnp.where(sub == i, r, out)
    return out


def main_kernel(
    hidden_hbm, gain_ref, head_hbm, pos_ref, tgt_ref, num_ref, den_ref,
    dl_out, normed_out, rg_out, gg_out, loss_out,
    hidden, head, slots, rows, lp, lrecv, e_all, cols,
    ss_y, ss_z, ss_x, ss_c, st_y, st_z, st_x, st_c,
    ubuf, crecv, xbuf, xrecv, zbuf, zrecv, rgall, ggz, ggx, ggc,
    load_sem,
    row_z_s, row_z_r, row_x_s, row_x_r, row_c_s, row_c_r,
    ss_s, ss_r, st_s, st_r, lg_s, lg_r, e_s, e_r,
    u_s, u_r, g_s, g_r, gg_s, gg_r,
):
    ctx = lax.axis_index("ctx")
    vy = lax.axis_index("vocab")
    x = ctx // 16
    z = (ctx // 2) % NZ
    k = ctx % 2
    voc = head.shape[0]

    def at_x(d):
        return (((x + d) % NX) * 16 + z * 2 + k, vy)

    def at_z(d):
        return (x * 16 + ((z + d) % NZ) * 2 + k, vy)

    def at_y(d):
        return (ctx, (vy + d) % NY)

    other = (x * 16 + z * 2 + (1 - k), vy)
    pair_d = 1 - 2 * (x % 2)
    pair = ((x + pair_d) * 16 + z * 2 + k, vy)

    load_hidden = pltpu.make_async_copy(hidden_hbm, hidden, load_sem.at[0])
    load_hidden.start()
    load_head = pltpu.make_async_copy(head_hbm, head, load_sem.at[1])
    load_head.start()

    barrier = pltpu.get_barrier_semaphore()
    peers = (
        [at_z(d) for d in range(1, NZ)]
        + [at_x(d) for d in range(1, NX)]
        + [at_y(d) for d in range(1, NY)]
        + [other]
    )
    for p in peers:
        pl.semaphore_signal(barrier, inc=1, device_id=p, device_id_type=MESH)

    def copy(src, dst, s, r, dev):
        return pltpu.make_async_remote_copy(
            src_ref=src, dst_ref=dst, send_sem=s, recv_sem=r, device_id=dev, device_id_type=MESH
        )

    sent = []

    def start(c):
        c.start()
        sent.append(c)
        return c

    pos = pos_ref[...].astype(F32)
    tgt = tgt_ref[...].astype(F32)
    pos_c = jnp.concatenate([column_of(pos[0:1]), column_of(pos[1:2]) + float(MODEL)], axis=0)
    tgt_c = jnp.concatenate([column_of(tgt[0:1]), column_of(tgt[1:2])], axis=0)
    cols[0] = jnp.broadcast_to(tgt_c, (ROWS, ROWS))
    pos_i = pos_c.astype(jnp.int32)
    owner_c = pos_i >> 8
    owner_l = lanes_of(owner_c.astype(F32))
    chosen = jnp.where(pos_i == ctx * TOK + iota((ROWS, TOK), 1), 1.0, 0.0)
    pick = jnp.sum(chosen.reshape(ROWS // 8, 8, TOK), axis=0).astype(BF16)
    load_hidden.wait()
    own = jnp.dot(pick, hidden[...], preferred_element_type=F32)
    half = WIDTH // 2
    slots[x, k, z] = jnp.concatenate([own[:, :half], own[:, half:]], axis=0).astype(BF16)
    squares = jnp.sum(own * own, axis=1, keepdims=True)
    lane8 = iota((8, ROWS), 1)
    mine = (lane8 % 8 == iota((8, ROWS), 0)) & (owner_l == ctx.astype(F32))
    ss = jnp.sum(jnp.where(mine, squares, 0.0), axis=0, keepdims=True)
    ss_y[vy] = jnp.broadcast_to(ss, (8, ROWS))

    pl.semaphore_wait(barrier, len(peers))

    def all_to_line(n, index, at, buf, ss_, rs_, base):
        cs = {}
        for d in range(1, n):
            cs[d] = start(copy(buf.at[index], buf.at[index], ss_.at[base + d], rs_.at[base + d], at(d)))
        return cs

    near = [1, 7, 2, 6, 3, 5, 4]
    cz = {}
    for d in [4, 3, 5, 2, 6, 1, 7]:
        cz[d] = start(copy(slots.at[x, k, z], slots.at[x, k, z], row_z_s.at[d], row_z_r.at[d], at_z(d)))
    cy = all_to_line(NY, vy, at_y, ss_y, ss_s, ss_r, 0)

    cx = {}

    def forward_x(d):
        zz = (z - d + NZ) % NZ
        for e in (2, 1, 3):
            cx[d, e] = start(
                copy(slots.at[x, k, zz], slots.at[x, k, zz], row_x_s.at[d, e], row_x_r.at[d, e], at_x(e))
            )

    forward_x(0)
    for d in near[:4]:
        cz[d].wait_recv()
        forward_x(d)
    for d in range(1, NY):
        cy[d].wait_recv()
    ss_z[z] = jnp.sum(ss_y[...], axis=0)
    cssz = all_to_line(NZ, z, at_z, ss_z, ss_s, ss_r, 8)
    for d in near[4:]:
        cz[d].wait_recv()
        forward_x(d)
    cc = {}

    def forward_core(e):
        xx = (x - e + NX) % NX
        cc[e] = start(copy(slots.at[xx, k], slots.at[xx, k], row_c_s.at[e], row_c_r.at[e], other))

    forward_core(0)
    for d in range(1, NZ):
        cssz[d].wait_recv()
    ss_x[x] = jnp.sum(ss_z[...], axis=0)
    cssx = all_to_line(NX, x, at_x, ss_x, ss_s, ss_r, 16)
    for e in (1, 3, 2):
        for d in range(NZ):
            cx[d, e].wait_recv()
        forward_core(e)
    for e in range(1, NX):
        cssx[e].wait_recv()
    ss_c[k] = jnp.sum(ss_x[...], axis=0)
    css = start(copy(ss_c.at[k], ss_c.at[k], ss_s.at[20], ss_r.at[20], other))
    for e in range(NX):
        cc[e].wait_recv()

    seq_block = owner_c - jnp.where(iota((ROWS, 1), 0) >= SEQ_ROWS, 32, 0)
    place = ((seq_block >> 4) * 16 + (seq_block & 1) * 8 + ((seq_block >> 1) & 7)) * 16 + (
        iota((ROWS, 1), 0) & 7
    )
    lane512 = iota((SEQ_ROWS, 512), 1)
    for s in range(2):
        here = place[s * SEQ_ROWS : (s + 1) * SEQ_ROWS]
        piece = slots[2 * s : 2 * s + 2].reshape(512, half)
        for h in range(2):
            spread = jnp.where(lane512 == here + 8 * h, 1.0, 0.0).astype(BF16)
            rows[s * SEQ_ROWS : (s + 1) * SEQ_ROWS, h * half : (h + 1) * half] = jnp.dot(
                spread, piece, preferred_element_type=F32
            )
    css.wait_recv()
    squares_l = (ss_c[0] + ss_c[1])[0:1]
    inv_l = lax.rsqrt(squares_l / float(MODEL) + EPSILON)
    inv_c = column_of(inv_l)
    cols[1] = jnp.broadcast_to(inv_c, (ROWS, ROWS))
    gain = gain_ref[...]
    normed = (rows[...] * inv_c * gain).astype(BF16)
    normed_out[...] = normed

    load_head.wait()
    lp[:, PADDED - 128 :] = jnp.zeros((ROWS, 128), F32)
    lp[:, :voc] = lax.dot_general(
        normed, head[...], (((1,), (1,)), ((), ())), preferred_element_type=F32
    )
    cl = {}
    for d in [4, 3, 5, 2, 6, 1, 7]:
        group = pl.ds(pl.multiple_of(((vy + d) % NY) * 16, 16), 16)
        cl[d] = start(copy(lp.at[group], lrecv.at[vy], lg_s.at[d], lg_r.at[d], at_y(d)))
    own_group = pl.ds(pl.multiple_of(vy * 16, 16), 16)
    lrecv[vy] = lp[own_group]
    for d in range(1, NY):
        cl[d].wait_recv()
    logits = lrecv[0]
    for i in range(1, NY):
        logits = logits + lrecv[i]

    lane = iota((16, PADDED), 1)
    live = lane < voc
    target = cols[0, own_group][:, 0:1].astype(jnp.int32) - ctx * voc
    top = jnp.max(jnp.where(live, logits, -jnp.inf), axis=1, keepdims=True)
    shifted = logits - top
    exps = jnp.where(live, jnp.exp(shifted), 0.0)
    e_all[own_group] = exps.astype(BF16)
    total = jnp.sum(exps, axis=1, keepdims=True)
    weighted = jnp.sum(exps * shifted, axis=1, keepdims=True)
    picked = jnp.sum(jnp.where(live & (lane == target), logits, 0.0), axis=1, keepdims=True)
    to_lane = iota((16, ROWS), 1) == vy * 16 + iota((16, ROWS), 0)
    st_y[vy] = stack_rows(
        *(jnp.sum(jnp.where(to_lane, v, 0.0), axis=0, keepdims=True) for v in (top, total, weighted, picked))
    )
    cy = all_to_line(NY, vy, at_y, st_y, st_s, st_r, 0)
    ce = {}
    for d in [4, 3, 5, 2, 6, 1, 7]:
        ce[d] = start(copy(e_all.at[own_group], e_all.at[own_group], e_s.at[d], e_r.at[d], at_y(d)))
    for d in range(1, NY):
        cy[d].wait_recv()
    block = jnp.sum(st_y[...], axis=0)
    st_z[z] = block
    cz = all_to_line(NZ, z, at_z, st_z, st_s, st_r, 8)
    for d in range(1, NZ):
        cz[d].wait_recv()
    st_x[x] = combine([st_z[i] for i in range(NZ)])
    cx = all_to_line(NX, x, at_x, st_x, st_s, st_r, 16)
    for d in range(1, NX):
        cx[d].wait_recv()
    st_c[k] = combine([st_x[i] for i in range(NX)])
    cst = start(copy(st_c.at[k], st_c.at[k], st_s.at[20], st_r.at[20], other))
    for d in range(1, NY):
        ce[d].wait_recv()
    cst.wait_recv()
    whole = combine([st_c[0], st_c[1]])

    lanes1 = iota((1, ROWS), 1)
    den = jnp.where(lanes1 < SEQ_ROWS, den_ref[0], den_ref[1]).astype(F32)
    num = jnp.where(lanes1 < SEQ_ROWS, num_ref[0], num_ref[1]).astype(F32)
    factor = den / (num * (2.0 * MODEL))
    log_total = whole[0:1] + jnp.log(whole[1:2])
    target_l = whole[3:4]
    loss = jnp.sum(factor * (log_total - target_l), axis=1, keepdims=True)
    loss_out[...] = jnp.broadcast_to(loss, (8, ROWS))
    scaled = LOSS_SCALE * factor
    w_c = column_of(scaled * jnp.exp(block[0:1] - log_total))
    t_c = column_of(scaled * (jnp.exp(target_l - log_total) - 1.0))
    inner = scaled * (whole[2:3] / whole[1:2] + (whole[0:1] - target_l)) / (inv_l * float(MODEL))
    cols[2] = jnp.broadcast_to(column_of(inv_l * inv_l * inv_l * inner), (ROWS, ROWS))
    is_target = iota((ROWS, PADDED), 1) + ctx * voc == tgt_c.astype(jnp.int32)
    is_target = is_target & (iota((ROWS, PADDED), 1) < voc)
    dl_out[...] = jnp.where(is_target, t_c, w_c * e_all[...].astype(F32)).astype(BF16)

    u = jnp.dot(dl_out[:, :voc], head[...], preferred_element_type=F32)
    for i in range(NX):
        for j in range(2):
            g = (i * 2 + j) * 16
            ubuf[j, i] = u[g : g + 16].astype(BF16)
    cu = start(copy(ubuf.at[1 - k], crecv, u_s.at[0], u_r.at[0], other))
    cu.wait_recv()
    xbuf[...] = (ubuf[k].astype(F32) + crecv[...].astype(F32)).astype(BF16)
    cu = {}
    for d in (2, 1, 3):
        cu[d] = start(copy(xbuf.at[(x + d) % NX], xrecv.at[x], u_s.at[d], u_r.at[d], at_x(d)))
    xrecv[x] = xbuf[x]
    for d in range(1, NX):
        cu[d].wait_recv()
    part = jnp.sum(xrecv[...].astype(F32), axis=0)
    for j in range(NZ):
        zbuf[j] = part[:, j * 128 : (j + 1) * 128].astype(BF16)
    cu = {}
    for d in [4, 3, 5, 2, 6, 1, 7]:
        cu[d] = start(copy(zbuf.at[(z + d) % NZ], zrecv.at[z], u_s.at[8 + d], u_r.at[8 + d], at_z(d)))
    zrecv[z] = zbuf[z]
    for d in range(1, NZ):
        cu[d].wait_recv()
    dn = jnp.sum(zrecv[...].astype(F32), axis=0)

    r0 = pl.ds(pl.multiple_of((x * 2 + k) * 16, 16), 16)
    c0 = pl.ds(pl.multiple_of(z * 128, 128), 128)
    rows_t = rows[r0, c0]
    inv_t = cols[1, r0]
    rg = inv_t * gain_ref[:, c0] * dn - rows_t * cols[2, r0]
    xl = x % 2
    rgall[k, xl, z] = rg.astype(BF16)
    ggz[z] = jnp.broadcast_to(jnp.sum(dn * rows_t * inv_t, axis=0, keepdims=True), (8, 128))
    cg = {}
    for d in [4, 3, 5, 2, 6, 1, 7]:
        cg[d] = start(copy(rgall.at[k, xl, z], rgall.at[k, xl, z], g_s.at[d], g_r.at[d], at_z(d)))
    cgg = all_to_line(NZ, z, at_z, ggz, gg_s, gg_r, 0)
    for d in range(1, NZ):
        cgg[d].wait_recv()
    sub = iota((8, 128), 0)
    gathered = jnp.zeros((8, 128), F32)
    for j in range(NZ):
        gathered = jnp.where(sub == j, ggz[j], gathered)
    ggx[x] = gathered
    cgg = all_to_line(NX, x, at_x, ggx, gg_s, gg_r, 8)
    for d in range(1, NZ):
        cg[d].wait_recv()
    cgx = start(copy(rgall.at[k, xl], rgall.at[k, xl], g_s.at[8], g_r.at[8], pair))
    for d in range(1, NX):
        cgg[d].wait_recv()
    ggc[k] = jnp.sum(ggx[...], axis=0)
    cgc = start(copy(ggc.at[k], ggc.at[k], gg_s.at[12], gg_r.at[12], other))
    cgx.wait_recv()
    cgr = start(copy(rgall.at[k], rgall.at[k], g_s.at[9], g_r.at[9], other))
    cgc.wait_recv()
    gg_out[...] = ggc[0] + ggc[1]
    cgr.wait_recv()
    for i in range(2):
        for j in range(2):
            g = (i * 2 + j) * 16
            for c in range(NZ):
                rg_out[g : g + 16, c * 128 : (c + 1) * 128] = rgall[j, i, c]
    for c in sent:
        c.wait_send()


def final_kernel(dl, normed, rg, pos_ref, gg, loss, gh_out, gx_out, gg_out, loss_out):
    ctx = lax.axis_index("ctx")
    voc = gh_out.shape[0]
    gh_out[...] = lax.dot_general(
        dl[:, :voc], normed[...], (((0,), (0,)), ((), ())), preferred_element_type=F32
    ).astype(BF16)
    pos = jnp.where(ctx < 32, pos_ref[0:1], pos_ref[1:2])
    local = pos - (ctx % 32) * TOK
    spread = jnp.where(iota((TOK, SEQ_ROWS), 0) == local, 1.0, 0.0).astype(BF16)
    gx_out[...] = jnp.dot(spread, rg[...], preferred_element_type=F32).astype(BF16)
    gg_out[...] = gg[...]
    loss_out[0, 0] = loss[0, 0]


def on_device(hidden, norm_gain, head, masked_pos, masked_targets, t_num, t_den):
    voc = head.shape[0]
    vm = pl.BlockSpec(memory_space=pltpu.VMEM)
    sm = pl.BlockSpec(memory_space=pltpu.SMEM)
    anyspace = pl.BlockSpec(memory_space=pl.ANY)
    V = pltpu.VMEM
    D = pltpu.SemaphoreType.DMA
    shape = jax.ShapeDtypeStruct
    dl, normed, rg, gg, loss = pl.pallas_call(
        main_kernel,
        name="main",
        out_shape=(
            shape((ROWS, PADDED), BF16),
            shape((ROWS, WIDTH), BF16),
            shape((SEQ_ROWS, WIDTH), BF16),
            shape((8, 128), F32),
            shape((8, 128), F32),
        ),
        in_specs=[anyspace, vm, anyspace, vm, vm, sm, sm],
        out_specs=(vm,) * 5,
        scratch_shapes=[
            V((TOK, WIDTH), BF16),
            V((voc, WIDTH), BF16),
            V((NX, 2, NZ, 16, WIDTH // 2), BF16),
            V((ROWS, WIDTH), F32),
            V((ROWS, PADDED), F32),
            V((NY, 16, PADDED), F32),
            V((ROWS, PADDED), BF16),
            V((3, ROWS, 128), F32),
            V((NY, 8, 128), F32),
            V((NZ, 8, 128), F32),
            V((NX, 8, 128), F32),
            V((2, 8, 128), F32),
            V((NY, 8, 128), F32),
            V((NZ, 8, 128), F32),
            V((NX, 8, 128), F32),
            V((2, 8, 128), F32),
            V((2, NX, 16, WIDTH), BF16),
            V((NX, 16, WIDTH), BF16),
            V((NX, 16, WIDTH), BF16),
            V((NX, 16, WIDTH), BF16),
            V((NZ, 16, 128), BF16),
            V((NZ, 16, 128), BF16),
            V((2, 2, NZ, 16, 128), BF16),
            V((NZ, 8, 128), F32),
            V((NX, 8, 128), F32),
            V((2, 8, 128), F32),
            D((2,)),
            D((8,)), D((8,)), D((8, 4)), D((8, 4)), D((4,)), D((4,)),
            D((24,)), D((24,)), D((24,)), D((24,)), D((8,)), D((8,)), D((8,)), D((8,)),
            D((16,)), D((16,)), D((16,)), D((16,)), D((16,)), D((16,)),
        ],
        compiler_params=pltpu.CompilerParams(
            collective_id=0, has_side_effects=True, vmem_limit_bytes=40 << 20
        ),
    )(hidden, norm_gain.reshape(1, WIDTH), head, masked_pos, masked_targets, t_num, t_den)
    grad_head, grad_hidden, grad_gain, loss_value = pl.pallas_call(
        final_kernel,
        name="final",
        out_shape=(
            shape((voc, WIDTH), BF16),
            shape((TOK, WIDTH), BF16),
            shape((8, 128), F32),
            shape((1, 1), F32),
        ),
        in_specs=[vm] * 6,
        out_specs=(vm, vm, vm, sm),
        compiler_params=pltpu.CompilerParams(vmem_limit_bytes=40 << 20),
    )(dl, normed, rg, masked_pos, gg, loss)
    return (loss_value.reshape(()), grad_hidden, grad_head, grad_gain.reshape(WIDTH))


def solution(mesh):
    placed = (P("ctx", "vocab"), P("vocab"), P("ctx", "vocab"), P(), P(), P(), P())
    return jax.shard_map(
        on_device,
        mesh=mesh,
        in_specs=placed,
        out_specs=(P(), P("ctx", "vocab"), P("ctx", "vocab"), P("vocab")),
        check_vma=False,
    )
```

time: 742 us -> 91.9 us (0.12)
  blocking collectives: 435 us -> 0 us
  waiting for transfers between devices: 247 us -> 0 us
  Pallas kernels: 0 us -> 85 us
  between operations: 15.9 us -> 0.66 us
  other arithmetic: 12.5 us -> 0 us
  local copies, waits for them, and re-layouts: 18.4 us -> 5.95 us
  matrix products: 10.3 us -> 0 us
    psum x4 -> x0, blocking collectives: 285 us -> none  [the longest x2 257 us: on_device(): lax.psum((jnp.sum(jnp.exp(logits - row_top[:, None]), axis=1), picked), '...]
    reduce_scatter x2 -> x0, waiting for transfers between devices: 159 us -> none  [the longest x1 138 us: on_device(): lax.psum_scatter(jnp.dot(all_grads, head, preferred_element_type=jnp.floa...]
    pmax x1 -> x0, blocking collectives: 129 us -> none  [on_device(): row_top = lax.pmax(local_top, 'ctx')]
    all_gather x1 -> x0, waiting for transfers between devices: 88.7 us -> none  [on_device(): normed_all = lax.all_gather(normed_own, 'ctx', axis=0, tiled=True)]
    pallas_call x0 -> x2, Pallas kernels: none -> 85 us  [the longest x1 82.8 us: on_device(): pl.pallas_call(main_kernel, name='main', out_shape=(shape((ROWS, PADDED),...]
    all_gather x1 -> x0, blocking collectives: 21.1 us -> none  [on_device(): all_grads = lax.all_gather(dlogits, 'vocab', axis=0, tiled=True)]
    gather x5 -> x0, local copies, waits for them, and re-layouts: 16.5 us -> none  [the longest x1 4.76 us: on_device(): offsets[owner_seq, owner_block] + lane_of]
    dot_general x3 -> x0, matrix products: 10.3 us -> none  [the longest x1 3.86 us: contract_last(): lax.dot_general(left, right, (((1,), (1,)), ((), ())), preferred_element_...]
  transfers between devices with their start and end apart: 3 -> 0, of which waited for: 3 -> 0; matrix products, arithmetic and copies ran while one was open for 3% -> 0% of each run, Pallas kernels for 0% -> 0%
where the time goes in v1:
time: 91.9 us; the launch traced here: 91.6 us
  Pallas kernels  85 us (92%)
  local copies, waits for them, and re-layouts  5.95 us (6%)
    pallas_call x1, Pallas kernels, on_device(): pl.pallas_call(main_kernel, name='main', out_shape=(shape((ROWS, PADDED),...  82.8 us
    unnamed x14, local copies, waits for them, and re-layouts  5.95 us
    pallas_call x1, Pallas kernels, on_device(): pl.pallas_call(final_kernel, name='final', out_shape=(shape((voc, WIDTH),...  2.19 us

profile of v1, /device:TPU:1, one launch (start us, length us, event | category | flops | bytes accessed | tf_op | source)
XLA Modules:
  0.0 91.6 jit_solution(14664038078649749182)
XLA Ops:
  0.6 0.0 copy-start
  0.6 1.6 %copy-done = bf16[988,1024]{1,0:T(8,128)(2,1)S(1)} copy-done((bf16[988,1024]{1,0:T(8,128)(2,1)S(1)}, bf16[988,1024]{1,0:T(8,128)(2,1)}, u32[]{:S(2)}) %copy-start) | copy-done | bytes 2023448
  2.2 0.0 copy-start.1
  2.2 1.0 %copy-done.1 = bf16[256,1024]{1,0:T(8,128)(2,1)S(1)} copy-done((bf16[256,1024]{1,0:T(8,128)(2,1)S(1)}, bf16[256,1024]{1,0:T(8,128)(2,1)}, u32[]{:S(2)}) %copy-start.1) | copy-done | bytes 524312
  3.2 0.0 copy-start.2
  3.2 0.7 copy-done.2
  3.9 0.0 copy-start.3
  3.9 0.7 copy-done.3
  4.6 0.0 copy-start.4
  4.6 0.7 copy-done.4
  5.3 0.0 copy-start.5
  5.3 0.7 copy-done.5
  5.9 0.0 copy-start.6
  5.9 0.7 copy-done.6
  6.6 82.8 %main.1 = (bf16[128,1024]{1,0:T(8,128)(2,1)S(1)}, bf16[128,1024]{1,0:T(8,128)(2,1)S(1)}, bf16[64,1024]{1,0:T(8,128)(2,1)S(1)}, f32[8,128]{1,0:T(8,128)S(1)}, f32[8,128]{1,0:T(8,128)S(1)}) custom-call(bf16[256,1024]{1,0:T(8,128)(2,1)S(1)} %copy-done.1, f32[1,1024]{1,0:T(1,128)S(1)} %bitcast.3, bf16[988,1024]{1,0:T(8,128)(2,1)S(1)} %copy-done, ...), custom_call_target="tpu_custom_call" | custom-call | tf_op jit(solution)/shard_map/main/pallas_call | solution.py:377
  89.4 2.2 %final.1 = (bf16[988,1024]{1,0:T(8,128)(2,1)}, bf16[256,1024]{1,0:T(8,128)(2,1)}, f32[8,128]{1,0:T(8,128)}, f32[1,1]{1,0:T(1,128)}) custom-call(bf16[128,1024]{1,0:T(8,128)(2,1)S(1)} %get-tuple-element.13.dl, bf16[128,1024]{1,0:T(8,128)(2,1)S(1)} %get-tuple-element.14.normed, bf16[64,1024]{1,0:T(8,128)(2,1)S(1)} %get-tuple-element.15.rg, ...), custom_call_target="tpu_custom_call" | custom-call | tf_op jit(solution)/shard_map/final/pallas_call | solution.py:425
Async XLA Ops:
  0.6 1.6 %copy-start = (bf16[988,1024]{1,0:T(8,128)(2,1)S(1)}, bf16[988,1024]{1,0:T(8,128)(2,1)}, u32[]{:S(2)}) copy-start(bf16[988,1024]{1,0:T(8,128)(2,1)} %head_hbm.1) | copy-start | bytes 6070276
  2.2 1.0 %copy-start.1 = (bf16[256,1024]{1,0:T(8,128)(2,1)S(1)}, bf16[256,1024]{1,0:T(8,128)(2,1)}, u32[]{:S(2)}) copy-start(bf16[256,1024]{1,0:T(8,128)(2,1)} %hidden_hbm.1) | copy-start | bytes 1572868
  3.2 0.7 copy-start.2
  3.9 0.7 copy-start.3
  4.6 0.7 copy-start.4
  5.3 0.7 copy-start.5
  5.9 0.7 copy-start.6

commit v2 on v1

v2 whole, which is shorter than its diff:
```python
import jax
import jax.numpy as jnp
from jax import lax
from jax.experimental import pallas as pl
from jax.experimental.pallas import tpu as pltpu
from jax.sharding import PartitionSpec as P

MESH = pl.DeviceIdType.MESH
F32 = jnp.float32
BF16 = jnp.bfloat16
EPSILON = 1e-05
LOSS_SCALE = 1024.0
NX, NZ, NY = 4, 8, 8
ROWS = 128
SEQ_ROWS = 64
TOK = 256
WIDTH = 1024
MODEL = 8192
HALF = 512
FAR_FIRST = (4, 3, 5, 2, 6, 1, 7)
NEAR_FIRST = (1, 7, 2, 6, 3, 5, 4)


def iota(shape, dim):
    return lax.broadcasted_iota(jnp.int32, shape, dim)


def column_of(lanes):
    n = lanes.shape[1]
    same = iota((n, n), 0) == iota((n, n), 1)
    return jnp.sum(jnp.where(same, lanes, 0.0), axis=1, keepdims=True)


def lanes_of(column):
    n = column.shape[0]
    same = iota((n, n), 0) == iota((n, n), 1)
    return jnp.sum(jnp.where(same, column, 0.0), axis=0, keepdims=True)


def combine(tiles):
    top = tiles[0][0:1]
    for t in tiles[1:]:
        top = jnp.maximum(top, t[0:1])
    total = weighted = picked = None
    for t in tiles:
        shift = t[0:1] - top
        scale = jnp.exp(shift)
        a = scale * t[1:2]
        b = scale * (t[2:3] + shift * t[1:2])
        c = t[3:4]
        total = a if total is None else total + a
        weighted = b if weighted is None else weighted + b
        picked = c if picked is None else picked + c
    return stack_rows(top, total, weighted, picked)


def stack_rows(*rows):
    sub = iota((8, ROWS), 0)
    out = jnp.zeros((8, ROWS), F32)
    for i, r in enumerate(rows):
        out = jnp.where(sub == i, r, out)
    return out


def main_kernel(
    hidden_hbm, gain_hbm, head_hbm, pos_hbm, tgt_hbm, num_hbm, den_hbm,
    dlt_out, normed_out, rg_out, small_out,
    hidden, gain_ref, head, pos_ref, tgt_ref, num_ref, den_ref,
    slots, rows, lp, lrecv, e_all, cols,
    ss_y, ss_z, ss_x, ss_c, st_y, st_z, st_x, st_c,
    ubuf, crecv, xbuf, xrecv, zbuf, zrecv, tbuf, tcrecv, txbuf, txrecv, rgall, ggz, ggx, ggc,
    dlt, normed_v, small, load_sem,
    row_z_s, row_z_r, row_x_s, row_x_r, row_c_s, row_c_r,
    ss_s, ss_r, st_s, st_r, lg_s, lg_r, e_s, e_r,
    u_s, u_r, t_s, t_r, g_s, g_r, gg_s, gg_r,
):
    ctx = lax.axis_index("ctx")
    vy = lax.axis_index("vocab")
    x = ctx // 16
    z = (ctx // 2) % NZ
    k = ctx % 2
    voc = head.shape[0]

    def at_x(d):
        return (((x + d) % NX) * 16 + z * 2 + k, vy)

    def at_z(d):
        return (x * 16 + ((z + d) % NZ) * 2 + k, vy)

    def at_y(d):
        return (ctx, (vy + d) % NY)

    pair_x = x + 1 - 2 * (x % 2)

    def at_pair(d):
        return (pair_x * 16 + ((z + d) % NZ) * 2 + k, vy)

    other = (x * 16 + z * 2 + (1 - k), vy)

    loads = []
    for i, (a, b) in enumerate(
        (
            (pos_hbm, pos_ref), (hidden_hbm, hidden), (tgt_hbm, tgt_ref), (gain_hbm, gain_ref),
            (num_hbm, num_ref), (den_hbm, den_ref), (head_hbm, head),
        )
    ):
        loads.append(pltpu.make_async_copy(a, b, load_sem.at[i]))
        loads[-1].start()
    load_head = loads[-1]

    barrier = pltpu.get_barrier_semaphore()
    peers = (
        [at_z(d) for d in range(1, NZ)]
        + [at_x(d) for d in range(1, NX)]
        + [at_pair(d) for d in range(1, NZ)]
        + [at_y(d) for d in range(1, NY)]
        + [other]
    )
    for p in peers:
        pl.semaphore_signal(barrier, inc=1, device_id=p, device_id_type=MESH)

    def copy(src, dst, s, r, dev):
        return pltpu.make_async_remote_copy(
            src_ref=src, dst_ref=dst, send_sem=s, recv_sem=r, device_id=dev, device_id_type=MESH
        )

    sent = []

    def start(c):
        c.start()
        sent.append(c)
        return c

    def to_line(order, index, at, buf, ss_, rs_, base):
        return {d: start(copy(buf.at[index], buf.at[index], ss_.at[base + d], rs_.at[base + d], at(d))) for d in order}

    def keep(i, lanes):
        c = column_of(lanes)
        cols[i] = jnp.broadcast_to(c, (ROWS, 128))
        return c

    for c in loads[:-1]:
        c.wait()
    pos = pos_ref[...].astype(F32)
    tgt = tgt_ref[...].astype(F32)
    pos_c = jnp.concatenate([column_of(pos[0:1]), column_of(pos[1:2]) + float(MODEL)], axis=0)
    tgt_c = jnp.concatenate([column_of(tgt[0:1]), column_of(tgt[1:2])], axis=0)
    cols[0] = jnp.broadcast_to(tgt_c, (ROWS, 128))
    tgt_c = tgt_c.astype(jnp.int32)
    pos_i = pos_c.astype(jnp.int32)
    owner_c = pos_i >> 8
    owner_l = lanes_of(owner_c.astype(F32))
    chosen = jnp.where(pos_i == ctx * TOK + iota((ROWS, TOK), 1), 1.0, 0.0)
    pick = jnp.sum(chosen.reshape(ROWS // 8, 8, TOK), axis=0).astype(BF16)
    own = jnp.dot(pick, hidden[...], preferred_element_type=F32)
    half = WIDTH // 2
    slots[x, k, z] = jnp.concatenate([own[:, :half], own[:, half:]], axis=0).astype(BF16)
    squares = jnp.sum(own * own, axis=1, keepdims=True)
    lane8 = iota((8, ROWS), 1)
    mine = (lane8 % 8 == iota((8, ROWS), 0)) & (owner_l == ctx.astype(F32))
    ss = jnp.sum(jnp.where(mine, squares, 0.0), axis=0, keepdims=True)
    ss_y[vy] = jnp.broadcast_to(ss, (8, ROWS))

    pl.semaphore_wait(barrier, len(peers))

    cz = to_line(FAR_FIRST, (x, k, z), at_z, slots, row_z_s, row_z_r, 0)
    cy = to_line(FAR_FIRST, vy, at_y, ss_y, ss_s, ss_r, 0)
    cx = {}

    def forward_x(d):
        zz = (z - d + NZ) % NZ
        for e in (2, 1, 3):
            cx[d, e] = start(
                copy(slots.at[x, k, zz], slots.at[x, k, zz], row_x_s.at[d, e], row_x_r.at[d, e], at_x(e))
            )

    forward_x(0)
    for d in NEAR_FIRST[:4]:
        cz[d].wait_recv()
        forward_x(d)
    for d in range(1, NY):
        cy[d].wait_recv()
    ss_z[z] = jnp.sum(ss_y[...], axis=0)
    cssz = to_line(FAR_FIRST, z, at_z, ss_z, ss_s, ss_r, 8)
    for d in NEAR_FIRST[4:]:
        cz[d].wait_recv()
        forward_x(d)
    cc = {}

    def forward_core(e):
        xx = (x - e + NX) % NX
        cc[e] = start(copy(slots.at[xx, k], slots.at[xx, k], row_c_s.at[e], row_c_r.at[e], other))

    forward_core(0)
    for d in range(1, NZ):
        cssz[d].wait_recv()
    ss_x[x] = jnp.sum(ss_z[...], axis=0)
    cssx = to_line((2, 1, 3), x, at_x, ss_x, ss_s, ss_r, 16)
    for e in (1, 3, 2):
        for d in range(NZ):
            cx[d, e].wait_recv()
        forward_core(e)
    for e in range(1, NX):
        cssx[e].wait_recv()
    ss_c[k] = jnp.sum(ss_x[...], axis=0)
    css = start(copy(ss_c.at[k], ss_c.at[k], ss_s.at[20], ss_r.at[20], other))
    for e in range(NX):
        cc[e].wait_recv()

    seq_block = owner_c - jnp.where(iota((ROWS, 1), 0) >= SEQ_ROWS, 32, 0)
    place = ((seq_block >> 4) * 16 + (seq_block & 1) * 8 + ((seq_block >> 1) & 7)) * 16 + (
        iota((ROWS, 1), 0) & 7
    )
    lane512 = iota((SEQ_ROWS, 512), 1)
    for s in range(2):
        here = place[s * SEQ_ROWS : (s + 1) * SEQ_ROWS]
        piece = slots[2 * s : 2 * s + 2].reshape(512, half)
        for h in range(2):
            spread = jnp.where(lane512 == here + 8 * h, 1.0, 0.0).astype(BF16)
            rows[s * SEQ_ROWS : (s + 1) * SEQ_ROWS, h * half : (h + 1) * half] = jnp.dot(
                spread, piece, preferred_element_type=F32
            )
    css.wait_recv()
    squares_l = (ss_c[0] + ss_c[1])[0:1]
    inv_l = lax.rsqrt(squares_l / float(MODEL) + EPSILON)
    inv_c = keep(1, inv_l)
    normed = (rows[...] * inv_c * gain_ref[...]).astype(BF16)
    normed_v[...] = normed
    stores = []

    def store(i, a, b):
        stores.append(pltpu.make_async_copy(a, b, load_sem.at[i]))
        stores[-1].start()

    store(0, normed_v, normed_out)

    load_head.wait()
    lives = (HALF, voc - HALF)
    head_part = (head.at[0:HALF], head.at[HALF:voc])
    own_group = pl.ds(pl.multiple_of(vy * 16, 16), 16)
    lp[1, :, HALF - 128 :] = jnp.zeros((ROWS, 128), F32)
    cl = {}
    for h in range(2):
        lp[h, :, : lives[h]] = lax.dot_general(
            normed, head_part[h][...], (((1,), (1,)), ((), ())), preferred_element_type=F32
        )
        for d in FAR_FIRST:
            group = pl.ds(pl.multiple_of(((vy + d) % NY) * 16, 16), 16)
            cl[h, d] = start(
                copy(lp.at[h, group], lrecv.at[h, vy], lg_s.at[8 * h + d], lg_r.at[8 * h + d], at_y(d))
            )
        lrecv[h, vy] = lp[h, own_group]

    is_target = []
    for h in range(2):
        entry = iota((ROWS, HALF), 1) + h * HALF
        is_target.append((entry + ctx * voc == tgt_c) & (entry < voc))

    def over_vocab(left):
        return sum(
            jnp.dot(left[h][:, : lives[h]], head_part[h][...], preferred_element_type=F32)
            for h in range(2)
        )

    def split(value, buf):
        for i in range(NX):
            for j in range(2):
                g = (i * 2 + j) * 16
                buf[j, i] = value[g : g + 16].astype(BF16)

    split(over_vocab([jnp.where(t, 1.0, 0.0).astype(BF16) for t in is_target]), tbuf)
    ct = start(copy(tbuf.at[1 - k], tcrecv, t_s.at[0], t_r.at[0], other))
    ct.wait_recv()
    txbuf[...] = (tbuf[k].astype(F32) + tcrecv[...].astype(F32)).astype(BF16)
    ct = {
        d: start(copy(txbuf.at[(x + d) % NX], txrecv.at[x], t_s.at[d], t_r.at[d], at_x(d)))
        for d in (2, 1, 3)
    }
    txrecv[x] = txbuf[x]

    to_lane = iota((16, ROWS), 1) == vy * 16 + iota((16, ROWS), 0)
    target16 = cols[0, own_group][:, 0:1].astype(jnp.int32) - ctx * voc
    stat_rows = []
    ce = {}
    for h in range(2):
        for d in range(1, NY):
            cl[h, d].wait_recv()
        logits = lrecv[h, 0]
        for i in range(1, NY):
            logits = logits + lrecv[h, i]
        lane = iota((16, HALF), 1)
        live = lane < lives[h]
        top = jnp.max(jnp.where(live, logits, -jnp.inf), axis=1, keepdims=True)
        shifted = logits - top
        exps = jnp.where(live, jnp.exp(shifted), 0.0)
        e_all[h, own_group] = exps.astype(BF16)
        stat = (
            top,
            jnp.sum(exps, axis=1, keepdims=True),
            jnp.sum(exps * shifted, axis=1, keepdims=True),
            jnp.sum(jnp.where(live & (lane + h * HALF == target16), logits, 0.0), axis=1, keepdims=True),
        )
        stat_rows += [jnp.sum(jnp.where(to_lane, v, 0.0), axis=0, keepdims=True) for v in stat]
        if h == 1:
            st_y[vy] = stack_rows(*stat_rows)
            cy = to_line(FAR_FIRST, vy, at_y, st_y, st_s, st_r, 0)
        for d in FAR_FIRST:
            ce[h, d] = start(
                copy(
                    e_all.at[h, own_group], e_all.at[h, own_group],
                    e_s.at[8 * h + d], e_r.at[8 * h + d], at_y(d),
                )
            )

    for d in range(1, NY):
        cy[d].wait_recv()
    block = jnp.sum(st_y[...], axis=0)
    tops = (block[0:1], block[4:5])
    st_c[k] = combine([block[0:4], block[4:8]])
    cst = start(copy(st_c.at[k], st_c.at[k], st_s.at[20], st_r.at[20], other))
    cst.wait_recv()
    by_core = combine([st_c[0], st_c[1]])
    st_x[x] = by_core
    cx = to_line((2, 1, 3), x, at_x, st_x, st_s, st_r, 16)

    u = None
    for h in range(2):
        scale = column_of(jnp.exp(tops[h] - by_core[0:1]))
        for d in range(1, NY):
            ce[h, d].wait_recv()
        left = jnp.where(is_target[h], 0.0, scale * e_all[h].astype(F32)).astype(BF16)
        part = jnp.dot(left[:, : lives[h]], head_part[h][...], preferred_element_type=F32)
        u = part if u is None else u + part
    split(u, ubuf)
    cu = start(copy(ubuf.at[1 - k], crecv, u_s.at[0], u_r.at[0], other))
    for d in range(1, NX):
        cx[d].wait_recv()
    by_x = combine([st_x[i] for i in range(NX)])
    st_z[z] = by_x
    cz = to_line(FAR_FIRST, z, at_z, st_z, st_s, st_r, 8)
    keep(3, jnp.exp(by_core[0:1] - by_x[0:1]))
    cu.wait_recv()
    for i in range(NX):
        scale = cols[3, pl.ds(pl.multiple_of((2 * i + k) * 16, 16), 16)][:, 0:1]
        xbuf[i] = (scale * (ubuf[k, i].astype(F32) + crecv[i].astype(F32))).astype(BF16)
    cu = {
        d: start(copy(xbuf.at[(x + d) % NX], xrecv.at[x], u_s.at[d], u_r.at[d], at_x(d)))
        for d in (2, 1, 3)
    }
    xrecv[x] = xbuf[x]
    for d in range(1, NZ):
        cz[d].wait_recv()
    whole = combine([st_z[i] for i in range(NZ)])

    lanes1 = iota((1, ROWS), 1)
    den = jnp.where(lanes1 < SEQ_ROWS, den_ref[0], den_ref[1]).astype(F32)
    num = jnp.where(lanes1 < SEQ_ROWS, num_ref[0], num_ref[1]).astype(F32)
    factor = den / (num * (2.0 * MODEL))
    log_total = whole[0:1] + jnp.log(whole[1:2])
    target_l = whole[3:4]
    scaled = LOSS_SCALE * factor
    t_c = keep(5, scaled * (jnp.exp(target_l - log_total) - 1.0))
    keep(4, scaled * jnp.exp(by_x[0:1] - log_total))
    r0 = pl.ds(pl.multiple_of((x * 2 + k) * 16, 16), 16)
    c0 = pl.ds(pl.multiple_of(z * 128, 128), 128)
    for d in range(1, NX):
        ct[d].wait_recv()
    of_targets = cols[5, r0][:, 0:1] * jnp.sum(txrecv[...].astype(F32), axis=0)
    for d in range(1, NX):
        cu[d].wait_recv()
    part = cols[4, r0][:, 0:1] * jnp.sum(xrecv[...].astype(F32), axis=0) + of_targets
    for j in range(NZ):
        zbuf[j] = part[:, j * 128 : (j + 1) * 128].astype(BF16)
    cu = {
        d: start(copy(zbuf.at[(z + d) % NZ], zrecv.at[z], u_s.at[8 + d], u_r.at[8 + d], at_z(d)))
        for d in FAR_FIRST
    }
    zrecv[z] = zbuf[z]
    gain_part = jnp.sum(part * rows[r0, :] * cols[1, r0][:, 0:1], axis=0, keepdims=True)
    ggz[z] = stack_rows(*(gain_part[:, j * 128 : (j + 1) * 128] for j in range(NZ)))
    cgg = to_line(FAR_FIRST, z, at_z, ggz, gg_s, gg_r, 0)

    loss = jnp.sum(factor * (log_total - target_l), axis=1, keepdims=True)
    small[8:16] = jnp.broadcast_to(loss, (8, ROWS))
    inner = scaled * (whole[2:3] / whole[1:2] + (whole[0:1] - target_l)) / (inv_l * float(MODEL))
    keep(2, inv_l * inv_l * inv_l * inner)
    for d in range(1, NZ):
        cu[d].wait_recv()
    dn = jnp.sum(zrecv[...].astype(F32), axis=0)
    rg = cols[1, r0] * gain_ref[:, c0] * dn - rows[r0, c0] * cols[2, r0]
    xl = x % 2
    rgall[xl, k, z] = rg.astype(BF16)
    mine = rgall.at[xl, k, z]
    cg = {}
    for d in FAR_FIRST:
        cg[d] = start(copy(mine, mine, g_s.at[d], g_r.at[d], at_z(d)))
    for d in FAR_FIRST + (0,):
        cg[8 + d] = start(copy(mine, mine, g_s.at[8 + d], g_r.at[8 + d], at_pair(d)))
    for d in range(1, NZ):
        cgg[d].wait_recv()
    ggx[x] = jnp.sum(ggz[...], axis=0)
    cgg = to_line((2, 1, 3), x, at_x, ggx, gg_s, gg_r, 8)
    for h in range(2):
        w_c = column_of(scaled * jnp.exp(tops[h] - log_total))
        dl = jnp.where(is_target[h], t_c, w_c * e_all[h].astype(F32))
        dlt[h * HALF : (h + 1) * HALF] = dl.T.astype(BF16)
    store(1, dlt, dlt_out)
    for d in range(1, NX):
        cgg[d].wait_recv()
    ggc[k] = jnp.sum(ggx[...], axis=0)
    cgc = start(copy(ggc.at[k], ggc.at[k], gg_s.at[12], gg_r.at[12], other))
    for c in cg.values():
        c.wait_recv()
    cgr = start(copy(rgall.at[:, k], rgall.at[:, k], g_s.at[16], g_r.at[16], other))
    cgc.wait_recv()
    small[0:8] = ggc[0] + ggc[1]
    store(2, small, small_out)
    for c in sent[:-1]:
        c.wait_send()
    cgr.wait_recv()
    store(3, rgall, rg_out)
    cgr.wait_send()
    for c in stores:
        c.wait()


def final_kernel(
    dlt_hbm, normed_hbm, rg_hbm, small_hbm, pos_hbm, gh_out, gx_out, gg_out, loss_out,
    dlt, normed, rg, small, pos_ref, gh, gx, sems,
):
    loads = []
    for i, (a, b) in enumerate(
        ((dlt_hbm, dlt), (normed_hbm, normed), (pos_hbm, pos_ref), (rg_hbm, rg), (small_hbm, small))
    ):
        loads.append(pltpu.make_async_copy(a, b, sems.at[i]))
        loads[-1].start()
    ctx = lax.axis_index("ctx")
    voc = gh.shape[0]
    for c in loads[:2]:
        c.wait()
    stores = []
    step = WIDTH // 4
    for i in range(4):
        c = slice(i * step, (i + 1) * step)
        gh[:, c] = jnp.dot(dlt[:voc], normed[:, c], preferred_element_type=F32).astype(BF16)
        stores.append(pltpu.make_async_copy(gh.at[:, c], gh_out.at[:, c], sems.at[8 + i]))
        stores[-1].start()
    for c in loads[2:]:
        c.wait()
    pos = jnp.where(ctx < 32, pos_ref[0:1], pos_ref[1:2])
    local = pos - (ctx % 32) * TOK
    spread = jnp.where(iota((TOK, SEQ_ROWS), 0) == local, 1.0, 0.0).astype(BF16)
    for j in range(NZ):
        piece = rg[:, :, j].reshape(SEQ_ROWS, 128)
        gx[:, j * 128 : (j + 1) * 128] = jnp.dot(spread, piece, preferred_element_type=F32).astype(BF16)
    stores.append(pltpu.make_async_copy(gx, gx_out, sems.at[5]))
    stores[-1].start()
    stores.append(pltpu.make_async_copy(small.at[0:8], gg_out, sems.at[6]))
    stores[-1].start()
    loss_out[0, 0] = small[8, 0]
    for c in stores:
        c.wait()


def on_device(hidden, norm_gain, head, masked_pos, masked_targets, t_num, t_den):
    voc = head.shape[0]
    sm = pl.BlockSpec(memory_space=pltpu.SMEM)
    hbm = pl.BlockSpec(memory_space=pltpu.HBM)
    V = pltpu.VMEM
    D = pltpu.SemaphoreType.DMA
    S = pltpu.SMEM
    I32 = jnp.int32
    shape = jax.ShapeDtypeStruct
    dlt, normed, rg, small = pl.pallas_call(
        main_kernel,
        name="main",
        out_shape=(
            shape((2 * HALF, ROWS), BF16),
            shape((ROWS, WIDTH), BF16),
            shape((2, 2, NZ, 16, 128), BF16),
            shape((16, 128), F32),
        ),
        in_specs=[hbm] * 7,
        out_specs=(hbm,) * 4,
        scratch_shapes=[
            V((TOK, WIDTH), BF16), V((1, WIDTH), F32), V((voc, WIDTH), BF16),
            V((2, SEQ_ROWS), I32), V((2, SEQ_ROWS), I32), S((2,), I32), S((2,), I32),
            V((NX, 2, NZ, 16, WIDTH // 2), BF16),
            V((ROWS, WIDTH), F32),
            V((2, ROWS, HALF), F32),
            V((2, NY, 16, HALF), F32),
            V((2, ROWS, HALF), BF16),
            V((6, ROWS, 128), F32),
            V((NY, 8, 128), F32), V((NZ, 8, 128), F32), V((NX, 8, 128), F32), V((2, 8, 128), F32),
            V((NY, 8, 128), F32), V((NZ, 8, 128), F32), V((NX, 8, 128), F32), V((2, 8, 128), F32),
            V((2, NX, 16, WIDTH), BF16), V((NX, 16, WIDTH), BF16),
            V((NX, 16, WIDTH), BF16), V((NX, 16, WIDTH), BF16),
            V((NZ, 16, 128), BF16), V((NZ, 16, 128), BF16),
            V((2, NX, 16, WIDTH), BF16), V((NX, 16, WIDTH), BF16),
            V((NX, 16, WIDTH), BF16), V((NX, 16, WIDTH), BF16),
            V((2, 2, NZ, 16, 128), BF16),
            V((NZ, 8, 128), F32), V((NX, 8, 128), F32), V((2, 8, 128), F32),
            V((2 * HALF, ROWS), BF16), V((ROWS, WIDTH), BF16), V((16, 128), F32),
            D((8,)),
            D((8,)), D((8,)), D((8, 4)), D((8, 4)), D((4,)), D((4,)),
            D((24,)), D((24,)), D((24,)), D((24,)), D((16,)), D((16,)), D((16,)), D((16,)),
            D((16,)), D((16,)), D((4,)), D((4,)), D((17,)), D((17,)), D((16,)), D((16,)),
        ],
        compiler_params=pltpu.CompilerParams(
            collective_id=0, has_side_effects=True, vmem_limit_bytes=60 << 20
        ),
    )(hidden, norm_gain.reshape(1, WIDTH), head, masked_pos, masked_targets, t_num, t_den)
    grad_head, grad_hidden, grad_gain, loss_value = pl.pallas_call(
        final_kernel,
        name="final",
        out_shape=(
            shape((voc, WIDTH), BF16),
            shape((TOK, WIDTH), BF16),
            shape((8, 128), F32),
            shape((1, 1), F32),
        ),
        in_specs=[hbm] * 5,
        out_specs=(hbm, hbm, hbm, sm),
        scratch_shapes=[
            V((2 * HALF, ROWS), BF16), V((ROWS, WIDTH), BF16), V((2, 2, NZ, 16, 128), BF16),
            V((16, 128), F32), V((2, SEQ_ROWS), I32),
            V((voc, WIDTH), BF16), V((TOK, WIDTH), BF16), D((12,)),
        ],
        compiler_params=pltpu.CompilerParams(vmem_limit_bytes=60 << 20),
    )(dlt, normed, rg, small, masked_pos)
    return (loss_value.reshape(()), grad_hidden, grad_head, grad_gain.reshape(WIDTH))


def solution(mesh):
    placed = (P("ctx", "vocab"), P("vocab"), P("ctx", "vocab"), P(), P(), P(), P())
    return jax.shard_map(
        on_device,
        mesh=mesh,
        in_specs=placed,
        out_specs=(P(), P("ctx", "vocab"), P("ctx", "vocab"), P("vocab")),
        check_vma=False,
    )
```

time: 91.9 us -> 76.9 us (0.84)
  Pallas kernels: 85 us -> 76.1 us
  local copies, waits for them, and re-layouts: 5.95 us -> 0 us
    pallas_call x1, Pallas kernels: 82.8 us -> 72.5 us  [on_device(): pl.pallas_call(main_kernel, name='main', out_shape=(shape((2 * HALF, ROWS...]
    unnamed x14 -> x0, local copies, waits for them, and re-layouts: 5.95 us -> none
    pallas_call x1, Pallas kernels: 2.19 us -> 3.59 us  [on_device(): pl.pallas_call(final_kernel, name='final', out_shape=(shape((voc, WIDTH),...]
where the time goes in v2:
time: 76.9 us; the launch traced here: 76.7 us
  Pallas kernels  76.1 us (99%)
    pallas_call x1, Pallas kernels, on_device(): pl.pallas_call(main_kernel, name='main', out_shape=(shape((2 * HALF, ROWS...  72.5 us
    pallas_call x1, Pallas kernels, on_device(): pl.pallas_call(final_kernel, name='final', out_shape=(shape((voc, WIDTH),...  3.59 us

profile of v2, /device:TPU:1, one launch (start us, length us, event | category | flops | bytes accessed | tf_op | source)
XLA Modules:
  0.0 76.7 jit_solution(9009958636682512909)
XLA Ops:
  0.6 72.5 %main.1 = (bf16[1024,128]{1,0:T(8,128)(2,1)}, bf16[128,1024]{1,0:T(8,128)(2,1)}, bf16[2,2,8,16,128]{4,3,2,1,0:T(8,128)(2,1)}, f32[16,128]{1,0:T(8,128)}) custom-call(bf16[256,1024]{1,0:T(8,128)(2,1)} %hidden_hbm.1, f32[1,1024]{1,0:T(1,128)} %bitcast.3, bf16[988,1024]{1,0:T(8,128)(2,1)} %head_hbm.1, s32[2,64]{1,0:T(2,128)} %pos_hbm.3, s32[2,64]{1,0:T(2,128)} %tgt_hbm.1, ...), custom_call_target="tpu_custom_call" | custom-call | tf_op jit(solution)/shard_map/main/pallas_call | solution.py:474
  73.1 3.6 %final.1 = (bf16[988,1024]{1,0:T(8,128)(2,1)}, bf16[256,1024]{1,0:T(8,128)(2,1)}, f32[8,128]{1,0:T(8,128)}, f32[1,1]{1,0:T(1,128)}) custom-call(bf16[1024,128]{1,0:T(8,128)(2,1)} %get-tuple-element.12.dlt_hbm, bf16[128,1024]{1,0:T(8,128)(2,1)} %get-tuple-element.13.normed_hbm, bf16[2,2,8,16,128]{4,3,2,1,0:T(8,128)(2,1)} %get-tuple-element.14.rg_hbm, ...), custom_call_target="tpu_custom_call" | custom-call | tf_op jit(solution)/shard_map/final/pallas_call | solution.py:513

commit v3 on v2

--- a/solution.py
+++ b/solution.py
@@ -28,6 +28,16 @@
 def column_of(lanes):
     n = lanes.shape[1]
     same = iota((n, n), 0) == iota((n, n), 1)
+    return jnp.sum(jnp.where(same, lanes, 0.0), axis=1, keepdims=True)
+
+
+def columns(*lanes):
+    turned = stack_rows(*lanes).T
+    return [turned[:, i : i + 1] for i in range(len(lanes))]
+
+
+def rows16(lanes, start):
+    same = iota((16, ROWS), 1) == start + iota((16, ROWS), 0)
     return jnp.sum(jnp.where(same, lanes, 0.0), axis=1, keepdims=True)
 
 
@@ -66,13 +76,13 @@
     hidden_hbm, gain_hbm, head_hbm, pos_hbm, tgt_hbm, num_hbm, den_hbm,
     dlt_out, normed_out, rg_out, small_out,
     hidden, gain_ref, head, pos_ref, tgt_ref, num_ref, den_ref,
-    slots, rows, lp, lrecv, e_all, cols,
-    ss_y, ss_z, ss_x, ss_c, st_y, st_z, st_x, st_c,
-    ubuf, crecv, xbuf, xrecv, zbuf, zrecv, tbuf, tcrecv, txbuf, txrecv, rgall, ggz, ggx, ggc,
+    slots, rows, lp, relay, relay4, lrecv, e_all,
+    ss_y, ss_p, ss_c, st_y, st_z, st_x, st_c,
+    ubuf, crecv, xbuf, xrecv, zbuf, zrecv, tbuf, tcrecv, txbuf, txrecv, tzbuf, tzrecv, rgall, gg_p, ggc,
     dlt, normed_v, small, load_sem,
     row_z_s, row_z_r, row_x_s, row_x_r, row_c_s, row_c_r,
-    ss_s, ss_r, st_s, st_r, lg_s, lg_r, e_s, e_r,
-    u_s, u_r, t_s, t_r, g_s, g_r, gg_s, gg_r,
+    ss_s, ss_r, ssp_s, ssp_r, st_s, st_r, rl_s, rl_r, lg_s, lg_r, e_s, e_r,
+    u_s, u_r, t_s, t_r, g_s, g_r, gg_s, gg_r, ggp_s, ggp_r,
 ):
     ctx = lax.axis_index("ctx")
     vy = lax.axis_index("vocab")
@@ -95,6 +105,10 @@
     def at_pair(d):
         return (pair_x * 16 + ((z + d) % NZ) * 2 + k, vy)
 
+    def at_xz(e, d):
+        return (((x + e) % NX) * 16 + ((z + d) % NZ) * 2 + k, vy)
+
+    plane = [(e, d) for d in FAR_FIRST + (0,) for e in (2, 1, 3, 0) if (e, d) != (0, 0)]
     other = (x * 16 + z * 2 + (1 - k), vy)
 
     loads = []
@@ -109,13 +123,7 @@
     load_head = loads[-1]
 
     barrier = pltpu.get_barrier_semaphore()
-    peers = (
-        [at_z(d) for d in range(1, NZ)]
-        + [at_x(d) for d in range(1, NX)]
-        + [at_pair(d) for d in range(1, NZ)]
-        + [at_y(d) for d in range(1, NY)]
-        + [other]
-    )
+    peers = [at_xz(e, d) for e, d in plane] + [at_y(d) for d in range(1, NY)] + [other]
     for p in peers:
         pl.semaphore_signal(barrier, inc=1, device_id=p, device_id_type=MESH)
 
@@ -134,10 +142,9 @@
     def to_line(order, index, at, buf, ss_, rs_, base):
         return {d: start(copy(buf.at[index], buf.at[index], ss_.at[base + d], rs_.at[base + d], at(d))) for d in order}
 
-    def keep(i, lanes):
-        c = column_of(lanes)
-        cols[i] = jnp.broadcast_to(c, (ROWS, 128))
-        return c
+    def to_plane(buf, ss_, rs_):
+        mine = buf.at[x, z]
+        return [start(copy(mine, mine, ss_.at[e, d], rs_.at[e, d], at_xz(e, d))) for e, d in plane]
 
     for c in loads[:-1]:
         c.wait()
@@ -145,7 +152,7 @@
     tgt = tgt_ref[...].astype(F32)
     pos_c = jnp.concatenate([column_of(pos[0:1]), column_of(pos[1:2]) + float(MODEL)], axis=0)
     tgt_c = jnp.concatenate([column_of(tgt[0:1]), column_of(tgt[1:2])], axis=0)
-    cols[0] = jnp.broadcast_to(tgt_c, (ROWS, 128))
+    tgt_l = lanes_of(tgt_c)
     tgt_c = tgt_c.astype(jnp.int32)
     pos_i = pos_c.astype(jnp.int32)
     owner_c = pos_i >> 8
@@ -159,7 +166,7 @@
     lane8 = iota((8, ROWS), 1)
     mine = (lane8 % 8 == iota((8, ROWS), 0)) & (owner_l == ctx.astype(F32))
     ss = jnp.sum(jnp.where(mine, squares, 0.0), axis=0, keepdims=True)
-    ss_y[vy] = jnp.broadcast_to(ss, (8, ROWS))
+    ss_y[vy] = ss
 
     pl.semaphore_wait(barrier, len(peers))
 
@@ -180,8 +187,8 @@
         forward_x(d)
     for d in range(1, NY):
         cy[d].wait_recv()
-    ss_z[z] = jnp.sum(ss_y[...], axis=0)
-    cssz = to_line(FAR_FIRST, z, at_z, ss_z, ss_s, ss_r, 8)
+    ss_p[x, z] = jnp.sum(ss_y[...], axis=0)
+    cssp = to_plane(ss_p, ssp_s, ssp_r)
     for d in NEAR_FIRST[4:]:
         cz[d].wait_recv()
         forward_x(d)
@@ -192,17 +199,13 @@
         cc[e] = start(copy(slots.at[xx, k], slots.at[xx, k], row_c_s.at[e], row_c_r.at[e], other))
 
     forward_core(0)
-    for d in range(1, NZ):
-        cssz[d].wait_recv()
-    ss_x[x] = jnp.sum(ss_z[...], axis=0)
-    cssx = to_line((2, 1, 3), x, at_x, ss_x, ss_s, ss_r, 16)
     for e in (1, 3, 2):
         for d in range(NZ):
             cx[d, e].wait_recv()
         forward_core(e)
-    for e in range(1, NX):
-        cssx[e].wait_recv()
-    ss_c[k] = jnp.sum(ss_x[...], axis=0)
+    for c in cssp:
+        c.wait_recv()
+    ss_c[k] = jnp.sum(ss_p[...].reshape(NX * NZ, 1, ROWS), axis=0)
     css = start(copy(ss_c.at[k], ss_c.at[k], ss_s.at[20], ss_r.at[20], other))
     for e in range(NX):
         cc[e].wait_recv()
@@ -221,9 +224,9 @@
                 spread, piece, preferred_element_type=F32
             )
     css.wait_recv()
-    squares_l = (ss_c[0] + ss_c[1])[0:1]
+    squares_l = ss_c[0] + ss_c[1]
     inv_l = lax.rsqrt(squares_l / float(MODEL) + EPSILON)
-    inv_c = keep(1, inv_l)
+    [inv_c] = columns(inv_l)
     normed = (rows[...] * inv_c * gain_ref[...]).astype(BF16)
     normed_v[...] = normed
     stores = []
@@ -239,17 +242,43 @@
     head_part = (head.at[0:HALF], head.at[HALF:voc])
     own_group = pl.ds(pl.multiple_of(vy * 16, 16), 16)
     lp[1, :, HALF - 128 :] = jnp.zeros((ROWS, 128), F32)
-    cl = {}
-    for h in range(2):
+
+    def group(d):
+        return pl.ds(pl.multiple_of(((vy + d) % NY) * 16, 16), 16)
+
+    ways = ((0, 1, 2, 3, slice(0, HALF // 2)), (1, 7, 6, 5, slice(HALF // 2, HALF)))
+    c1 = {}
+
+    def first_sends(h):
         lp[h, :, : lives[h]] = lax.dot_general(
             normed, head_part[h][...], (((1,), (1,)), ((), ())), preferred_element_type=F32
         )
-        for d in FAR_FIRST:
-            group = pl.ds(pl.multiple_of(((vy + d) % NY) * 16, 16), 16)
-            cl[h, d] = start(
-                copy(lp.at[h, group], lrecv.at[h, vy], lg_s.at[8 * h + d], lg_r.at[8 * h + d], at_y(d))
-            )
-        lrecv[h, vy] = lp[h, own_group]
+        for w, _, two, three, part4 in ways:
+            i = 4 * h + 2 * w
+            c1[h, w, 0] = start(
+                copy(lp.at[h, group(4), part4], relay4.at[h, w], rl_s.at[i], rl_r.at[i], at_y(two))
+            )
+            c1[h, w, 1] = start(
+                copy(lp.at[h, group(three)], relay.at[h, w], rl_s.at[i + 1], rl_r.at[i + 1], at_y(two))
+            )
+
+    first_sends(0)
+    first_sends(1)
+    cl = {}
+
+    def pass_on(h):
+        for w, one, two, _, part4 in ways:
+            i = 4 * h + 2 * w
+            c1[h, w, 0].wait_recv()
+            lp[h, group(two), part4] += relay4[h, w]
+            cl[h, w, 0] = start(
+                copy(lp.at[h, group(two)], lrecv.at[h, 2 * w], lg_s.at[i], lg_r.at[i], at_y(two))
+            )
+            c1[h, w, 1].wait_recv()
+            lp[h, group(one)] += relay[h, w]
+            cl[h, w, 1] = start(
+                copy(lp.at[h, group(one)], lrecv.at[h, 2 * w + 1], lg_s.at[i + 1], lg_r.at[i + 1], at_y(one))
+            )
 
     is_target = []
     for h in range(2):
@@ -277,16 +306,29 @@
         for d in (2, 1, 3)
     }
     txrecv[x] = txbuf[x]
+    pass_on(0)
+    pass_on(1)
+    for d in range(1, NX):
+        ct[d].wait_recv()
+    of_targets = jnp.sum(txrecv[...].astype(F32), axis=0)
+    for j in range(NZ):
+        tzbuf[j] = of_targets[:, j * 128 : (j + 1) * 128].astype(BF16)
+    ct = {
+        d: start(copy(tzbuf.at[(z + d) % NZ], tzrecv.at[z], t_s.at[8 + d], t_r.at[8 + d], at_z(d)))
+        for d in FAR_FIRST
+    }
+    tzrecv[z] = tzbuf[z]
 
     to_lane = iota((16, ROWS), 1) == vy * 16 + iota((16, ROWS), 0)
-    target16 = cols[0, own_group][:, 0:1].astype(jnp.int32) - ctx * voc
+    target16 = rows16(tgt_l, vy * 16).astype(jnp.int32) - ctx * voc
     stat_rows = []
     ce = {}
     for h in range(2):
-        for d in range(1, NY):
-            cl[h, d].wait_recv()
-        logits = lrecv[h, 0]
-        for i in range(1, NY):
+        for w in range(2):
+            cl[h, w, 0].wait_recv()
+            cl[h, w, 1].wait_recv()
+        logits = lp[h, own_group]
+        for i in range(4):
             logits = logits + lrecv[h, i]
         lane = iota((16, HALF), 1)
         live = lane < lives[h]
@@ -316,38 +358,58 @@
         cy[d].wait_recv()
     block = jnp.sum(st_y[...], axis=0)
     tops = (block[0:1], block[4:5])
-    st_c[k] = combine([block[0:4], block[4:8]])
+    here = combine([block[0:4], block[4:8]])
+    st_c[k] = here
     cst = start(copy(st_c.at[k], st_c.at[k], st_s.at[20], st_r.at[20], other))
+
+    u = None
+    scales = columns(jnp.exp(tops[0] - here[0:1]), jnp.exp(tops[1] - here[0:1]))
+    for h in range(2):
+        for d in range(1, NY):
+            ce[h, d].wait_recv()
+        left = jnp.where(is_target[h], 0.0, scales[h] * e_all[h].astype(F32)).astype(BF16)
+        part = jnp.dot(left[:, : lives[h]], head_part[h][...], preferred_element_type=F32)
+        u = part if u is None else u + part
+    split(u, ubuf)
+    cu = start(copy(ubuf.at[1 - k], crecv, u_s.at[0], u_r.at[0], other))
     cst.wait_recv()
     by_core = combine([st_c[0], st_c[1]])
     st_x[x] = by_core
     cx = to_line((2, 1, 3), x, at_x, st_x, st_s, st_r, 16)
-
-    u = None
-    for h in range(2):
-        scale = column_of(jnp.exp(tops[h] - by_core[0:1]))
-        for d in range(1, NY):
-            ce[h, d].wait_recv()
-        left = jnp.where(is_target[h], 0.0, scale * e_all[h].astype(F32)).astype(BF16)
-        part = jnp.dot(left[:, : lives[h]], head_part[h][...], preferred_element_type=F32)
-        u = part if u is None else u + part
-    split(u, ubuf)
-    cu = start(copy(ubuf.at[1 - k], crecv, u_s.at[0], u_r.at[0], other))
+    own_l = jnp.exp(here[0:1] - by_core[0:1])
+    other_l = jnp.exp(st_c[1 - k][0:1] - by_core[0:1])
+    own_s = [rows16(own_l, (2 * i + k) * 16) for i in range(NX)]
+    other_s = [rows16(other_l, (2 * i + k) * 16) for i in range(NX)]
+    cu.wait_recv()
+    for i in range(NX):
+        xbuf[i] = (own_s[i] * ubuf[k, i].astype(F32) + other_s[i] * crecv[i].astype(F32)).astype(BF16)
+    cu = {
+        d: start(copy(xbuf.at[(x + d) % NX], xrecv.at[x], u_s.at[d], u_r.at[d], at_x(d)))
+        for d in (2, 1, 3)
+    }
+    xrecv[x] = xbuf[x]
     for d in range(1, NX):
         cx[d].wait_recv()
     by_x = combine([st_x[i] for i in range(NX)])
     st_z[z] = by_x
     cz = to_line(FAR_FIRST, z, at_z, st_z, st_s, st_r, 8)
-    keep(3, jnp.exp(by_core[0:1] - by_x[0:1]))
-    cu.wait_recv()
-    for i in range(NX):
-        scale = cols[3, pl.ds(pl.multiple_of((2 * i + k) * 16, 16), 16)][:, 0:1]
-        xbuf[i] = (scale * (ubuf[k, i].astype(F32) + crecv[i].astype(F32))).astype(BF16)
+    first = (x * 2 + k) * 16
+    r0 = pl.ds(pl.multiple_of(first, 16), 16)
+    c0 = pl.ds(pl.multiple_of(z * 128, 128), 128)
+    scales = [rows16(jnp.exp(st_x[i][0:1] - by_x[0:1]), first) for i in range(NX)]
+    inv16 = rows16(inv_l, first)
+    for d in range(1, NX):
+        cu[d].wait_recv()
+    part = scales[0] * xrecv[0].astype(F32)
+    for i in range(1, NX):
+        part = part + scales[i] * xrecv[i].astype(F32)
+    for j in range(NZ):
+        zbuf[j] = part[:, j * 128 : (j + 1) * 128].astype(BF16)
     cu = {
-        d: start(copy(xbuf.at[(x + d) % NX], xrecv.at[x], u_s.at[d], u_r.at[d], at_x(d)))
-        for d in (2, 1, 3)
+        d: start(copy(zbuf.at[(z + d) % NZ], zrecv.at[z], u_s.at[8 + d], u_r.at[8 + d], at_z(d)))
+        for d in FAR_FIRST
     }
-    xrecv[x] = xbuf[x]
+    zrecv[z] = zbuf[z]
     for d in range(1, NZ):
         cz[d].wait_recv()
     whole = combine([st_z[i] for i in range(NZ)])
@@ -359,35 +421,29 @@
     log_total = whole[0:1] + jnp.log(whole[1:2])
     target_l = whole[3:4]
     scaled = LOSS_SCALE * factor
-    t_c = keep(5, scaled * (jnp.exp(target_l - log_total) - 1.0))
-    keep(4, scaled * jnp.exp(by_x[0:1] - log_total))
-    r0 = pl.ds(pl.multiple_of((x * 2 + k) * 16, 16), 16)
-    c0 = pl.ds(pl.multiple_of(z * 128, 128), 128)
-    for d in range(1, NX):
-        ct[d].wait_recv()
-    of_targets = cols[5, r0][:, 0:1] * jnp.sum(txrecv[...].astype(F32), axis=0)
-    for d in range(1, NX):
-        cu[d].wait_recv()
-    part = cols[4, r0][:, 0:1] * jnp.sum(xrecv[...].astype(F32), axis=0) + of_targets
-    for j in range(NZ):
-        zbuf[j] = part[:, j * 128 : (j + 1) * 128].astype(BF16)
-    cu = {
-        d: start(copy(zbuf.at[(z + d) % NZ], zrecv.at[z], u_s.at[8 + d], u_r.at[8 + d], at_z(d)))
-        for d in FAR_FIRST
-    }
-    zrecv[z] = zbuf[z]
-    gain_part = jnp.sum(part * rows[r0, :] * cols[1, r0][:, 0:1], axis=0, keepdims=True)
-    ggz[z] = stack_rows(*(gain_part[:, j * 128 : (j + 1) * 128] for j in range(NZ)))
-    cgg = to_line(FAR_FIRST, z, at_z, ggz, gg_s, gg_r, 0)
+    t_l = scaled * (jnp.exp(target_l - log_total) - 1.0)
+    t16 = rows16(t_l, first)
+    part = rows16(scaled * jnp.exp(by_x[0:1] - log_total), first) * part + t16 * of_targets
+    gain_part = jnp.sum(part * rows[r0, :] * inv16, axis=0, keepdims=True)
+    gg_p[x, z] = stack_rows(*(gain_part[:, j * 128 : (j + 1) * 128] for j in range(NZ)))
+    cgg = to_plane(gg_p, ggp_s, ggp_r)
 
     loss = jnp.sum(factor * (log_total - target_l), axis=1, keepdims=True)
     small[8:16] = jnp.broadcast_to(loss, (8, ROWS))
+    scales = [rows16(scaled * jnp.exp(st_z[i][0:1] - log_total), first) for i in range(NZ)]
     inner = scaled * (whole[2:3] / whole[1:2] + (whole[0:1] - target_l)) / (inv_l * float(MODEL))
-    keep(2, inv_l * inv_l * inv_l * inner)
+    inner16 = rows16(inv_l * inv_l * inv_l * inner, first)
+    for d in range(1, NZ):
+        ct[d].wait_recv()
+    of_targets = t16 * jnp.sum(tzrecv[...].astype(F32), axis=0)
+    turned = inv16 * gain_ref[:, c0]
+    taken = rows[r0, c0] * inner16
     for d in range(1, NZ):
         cu[d].wait_recv()
-    dn = jnp.sum(zrecv[...].astype(F32), axis=0)
-    rg = cols[1, r0] * gain_ref[:, c0] * dn - rows[r0, c0] * cols[2, r0]
+    dn = of_targets
+    for i in range(NZ):
+        dn = dn + scales[i] * zrecv[i].astype(F32)
+    rg = turned * dn - taken
     xl = x % 2
     rgall[xl, k, z] = rg.astype(BF16)
     mine = rgall.at[xl, k, z]
@@ -396,19 +452,15 @@
         cg[d] = start(copy(mine, mine, g_s.at[d], g_r.at[d], at_z(d)))
     for d in FAR_FIRST + (0,):
         cg[8 + d] = start(copy(mine, mine, g_s.at[8 + d], g_r.at[8 + d], at_pair(d)))
-    for d in range(1, NZ):
-        cgg[d].wait_recv()
-    ggx[x] = jnp.sum(ggz[...], axis=0)
-    cgg = to_line((2, 1, 3), x, at_x, ggx, gg_s, gg_r, 8)
+    t_c, *w_c = columns(t_l, *(scaled * jnp.exp(t - log_total) for t in tops))
     for h in range(2):
-        w_c = column_of(scaled * jnp.exp(tops[h] - log_total))
-        dl = jnp.where(is_target[h], t_c, w_c * e_all[h].astype(F32))
+        dl = jnp.where(is_target[h], t_c, w_c[h] * e_all[h].astype(F32))
         dlt[h * HALF : (h + 1) * HALF] = dl.T.astype(BF16)
     store(1, dlt, dlt_out)
-    for d in range(1, NX):
-        cgg[d].wait_recv()
-    ggc[k] = jnp.sum(ggx[...], axis=0)
-    cgc = start(copy(ggc.at[k], ggc.at[k], gg_s.at[12], gg_r.at[12], other))
+    for c in cgg:
+        c.wait_recv()
+    ggc[k] = jnp.sum(gg_p[...].reshape(NX * NZ, 8, 128), axis=0)
+    cgc = start(copy(ggc.at[k], ggc.at[k], gg_s.at[0], gg_r.at[0], other))
     for c in cg.values():
         c.wait_recv()
     cgr = start(copy(rgall.at[:, k], rgall.at[:, k], g_s.at[16], g_r.at[16], other))
@@ -488,23 +540,25 @@
             V((NX, 2, NZ, 16, WIDTH // 2), BF16),
             V((ROWS, WIDTH), F32),
             V((2, ROWS, HALF), F32),
-            V((2, NY, 16, HALF), F32),
+            V((2, 2, 16, HALF), F32),
+            V((2, 2, 16, HALF // 2), F32),
+            V((2, 4, 16, HALF), F32),
             V((2, ROWS, HALF), BF16),
-            V((6, ROWS, 128), F32),
-            V((NY, 8, 128), F32), V((NZ, 8, 128), F32), V((NX, 8, 128), F32), V((2, 8, 128), F32),
+            V((NY, 1, 128), F32), V((NX, NZ, 1, 128), F32), V((2, 1, 128), F32),
             V((NY, 8, 128), F32), V((NZ, 8, 128), F32), V((NX, 8, 128), F32), V((2, 8, 128), F32),
             V((2, NX, 16, WIDTH), BF16), V((NX, 16, WIDTH), BF16),
             V((NX, 16, WIDTH), BF16), V((NX, 16, WIDTH), BF16),
             V((NZ, 16, 128), BF16), V((NZ, 16, 128), BF16),
             V((2, NX, 16, WIDTH), BF16), V((NX, 16, WIDTH), BF16),
             V((NX, 16, WIDTH), BF16), V((NX, 16, WIDTH), BF16),
+            V((NZ, 16, 128), BF16), V((NZ, 16, 128), BF16),
             V((2, 2, NZ, 16, 128), BF16),
-            V((NZ, 8, 128), F32), V((NX, 8, 128), F32), V((2, 8, 128), F32),
+            V((NX, NZ, 8, 128), F32), V((2, 8, 128), F32),
             V((2 * HALF, ROWS), BF16), V((ROWS, WIDTH), BF16), V((16, 128), F32),
             D((8,)),
             D((8,)), D((8,)), D((8, 4)), D((8, 4)), D((4,)), D((4,)),
-            D((24,)), D((24,)), D((24,)), D((24,)), D((16,)), D((16,)), D((16,)), D((16,)),
-            D((16,)), D((16,)), D((4,)), D((4,)), D((17,)), D((17,)), D((16,)), D((16,)),
+            D((24,)), D((24,)), D((NX, NZ)), D((NX, NZ)), D((24,)), D((24,)), D((8,)), D((8,)), D((8,)), D((8,)), D((16,)), D((16,)),
+            D((16,)), D((16,)), D((16,)), D((16,)), D((17,)), D((17,)), D((1,)), D((1,)), D((NX, NZ)), D((NX, NZ)),
         ],
         compiler_params=pltpu.CompilerParams(
             collective_id=0, has_side_effects=True, vmem_limit_bytes=60 << 20

time: 76.9 us -> 74.4 us (0.967)
  Pallas kernels: 76.1 us -> 73.6 us
    pallas_call x1, Pallas kernels: 72.5 us -> 70 us  [on_device(): pl.pallas_call(main_kernel, name='main', out_shape=(shape((2 * HALF, ROWS...]
where the time goes in v3:
time: 74.4 us; the launch traced here: 74.2 us
  Pallas kernels  73.6 us (99%)
    pallas_call x1, Pallas kernels, on_device(): pl.pallas_call(main_kernel, name='main', out_shape=(shape((2 * HALF, ROWS...  70 us
    pallas_call x1, Pallas kernels, on_device(): pl.pallas_call(final_kernel, name='final', out_shape=(shape((voc, WIDTH),...  3.57 us

profile of v3, /device:TPU:1, one launch (start us, length us, event | category | flops | bytes accessed | tf_op | source)
XLA Modules:
  0.0 74.2 jit_solution(16327339482871714238)
XLA Ops:
  0.6 70.0 %main.1 = (bf16[1024,128]{1,0:T(8,128)(2,1)}, bf16[128,1024]{1,0:T(8,128)(2,1)}, bf16[2,2,8,16,128]{4,3,2,1,0:T(8,128)(2,1)}, f32[16,128]{1,0:T(8,128)}) custom-call(bf16[256,1024]{1,0:T(8,128)(2,1)} %hidden_hbm.1, f32[1,1024]{1,0:T(1,128)} %bitcast.3, bf16[988,1024]{1,0:T(8,128)(2,1)} %head_hbm.1, s32[2,64]{1,0:T(2,128)} %pos_hbm.3, s32[2,64]{1,0:T(2,128)} %tgt_hbm.1, ...), custom_call_target="tpu_custom_call" | custom-call | tf_op jit(solution)/shard_map/main/pallas_call | solution.py:526
  70.7 3.6 %final.1 = (bf16[988,1024]{1,0:T(8,128)(2,1)}, bf16[256,1024]{1,0:T(8,128)(2,1)}, f32[8,128]{1,0:T(8,128)}, f32[1,1]{1,0:T(1,128)}) custom-call(bf16[1024,128]{1,0:T(8,128)(2,1)} %get-tuple-element.12.dlt_hbm, bf16[128,1024]{1,0:T(8,128)(2,1)} %get-tuple-element.13.normed_hbm, bf16[2,2,8,16,128]{4,3,2,1,0:T(8,128)(2,1)} %get-tuple-element.14.rg_hbm, ...), custom_call_target="tpu_custom_call" | custom-call | tf_op jit(solution)/shard_map/final/pallas_call | solution.py:567

commit v4 on v3

--- a/solution.py
+++ b/solution.py
@@ -77,11 +77,11 @@
     dlt_out, normed_out, rg_out, small_out,
     hidden, gain_ref, head, pos_ref, tgt_ref, num_ref, den_ref,
     slots, rows, lp, relay, relay4, lrecv, e_all,
-    ss_y, ss_p, ss_c, st_y, st_z, st_x, st_c,
+    ss_y, ss_z, ss_x, ss_c, st_y, st_z, st_x, st_c,
     ubuf, crecv, xbuf, xrecv, zbuf, zrecv, tbuf, tcrecv, txbuf, txrecv, tzbuf, tzrecv, rgall, gg_p, ggc,
     dlt, normed_v, small, load_sem,
     row_z_s, row_z_r, row_x_s, row_x_r, row_c_s, row_c_r,
-    ss_s, ss_r, ssp_s, ssp_r, st_s, st_r, rl_s, rl_r, lg_s, lg_r, e_s, e_r,
+    ss_s, ss_r, st_s, st_r, rl_s, rl_r, lg_s, lg_r, e_s, e_r,
     u_s, u_r, t_s, t_r, g_s, g_r, gg_s, gg_r, ggp_s, ggp_r,
 ):
     ctx = lax.axis_index("ctx")
@@ -110,6 +110,16 @@
 
     plane = [(e, d) for d in FAR_FIRST + (0,) for e in (2, 1, 3, 0) if (e, d) != (0, 0)]
     other = (x * 16 + z * 2 + (1 - k), vy)
+
+    barrier = pltpu.get_barrier_semaphore()
+    peers = (
+        [at_z(d) for d in FAR_FIRST]
+        + [at_y(d) for d in FAR_FIRST]
+        + [at_x(d) for d in (2, 1, 3)]
+        + [other]
+    )
+    for p in peers:
+        pl.semaphore_signal(barrier, inc=1, device_id=p, device_id_type=MESH)
 
     loads = []
     for i, (a, b) in enumerate(
@@ -121,11 +131,6 @@
         loads.append(pltpu.make_async_copy(a, b, load_sem.at[i]))
         loads[-1].start()
     load_head = loads[-1]
-
-    barrier = pltpu.get_barrier_semaphore()
-    peers = [at_xz(e, d) for e, d in plane] + [at_y(d) for d in range(1, NY)] + [other]
-    for p in peers:
-        pl.semaphore_signal(barrier, inc=1, device_id=p, device_id_type=MESH)
 
     def copy(src, dst, s, r, dev):
         return pltpu.make_async_remote_copy(
@@ -187,8 +192,8 @@
         forward_x(d)
     for d in range(1, NY):
         cy[d].wait_recv()
-    ss_p[x, z] = jnp.sum(ss_y[...], axis=0)
-    cssp = to_plane(ss_p, ssp_s, ssp_r)
+    ss_z[z] = jnp.sum(ss_y[...], axis=0)
+    cssz = to_line(FAR_FIRST, z, at_z, ss_z, ss_s, ss_r, 8)
     for d in NEAR_FIRST[4:]:
         cz[d].wait_recv()
         forward_x(d)
@@ -199,13 +204,17 @@
         cc[e] = start(copy(slots.at[xx, k], slots.at[xx, k], row_c_s.at[e], row_c_r.at[e], other))
 
     forward_core(0)
+    for d in range(1, NZ):
+        cssz[d].wait_recv()
+    ss_x[x] = jnp.sum(ss_z[...], axis=0)
+    cssx = to_line((2, 1, 3), x, at_x, ss_x, ss_s, ss_r, 16)
     for e in (1, 3, 2):
         for d in range(NZ):
             cx[d, e].wait_recv()
         forward_core(e)
-    for c in cssp:
-        c.wait_recv()
-    ss_c[k] = jnp.sum(ss_p[...].reshape(NX * NZ, 1, ROWS), axis=0)
+    for e in range(1, NX):
+        cssx[e].wait_recv()
+    ss_c[k] = jnp.sum(ss_x[...], axis=0)
     css = start(copy(ss_c.at[k], ss_c.at[k], ss_s.at[20], ss_r.at[20], other))
     for e in range(NX):
         cc[e].wait_recv()
@@ -544,7 +553,7 @@
             V((2, 2, 16, HALF // 2), F32),
             V((2, 4, 16, HALF), F32),
             V((2, ROWS, HALF), BF16),
-            V((NY, 1, 128), F32), V((NX, NZ, 1, 128), F32), V((2, 1, 128), F32),
+            V((NY, 1, 128), F32), V((NZ, 1, 128), F32), V((NX, 1, 128), F32), V((2, 1, 128), F32),
             V((NY, 8, 128), F32), V((NZ, 8, 128), F32), V((NX, 8, 128), F32), V((2, 8, 128), F32),
             V((2, NX, 16, WIDTH), BF16), V((NX, 16, WIDTH), BF16),
             V((NX, 16, WIDTH), BF16), V((NX, 16, WIDTH), BF16),
@@ -557,7 +566,7 @@
             V((2 * HALF, ROWS), BF16), V((ROWS, WIDTH), BF16), V((16, 128), F32),
             D((8,)),
             D((8,)), D((8,)), D((8, 4)), D((8, 4)), D((4,)), D((4,)),
-            D((24,)), D((24,)), D((NX, NZ)), D((NX, NZ)), D((24,)), D((24,)), D((8,)), D((8,)), D((8,)), D((8,)), D((16,)), D((16,)),
+            D((24,)), D((24,)), D((24,)), D((24,)), D((8,)), D((8,)), D((8,)), D((8,)), D((16,)), D((16,)),
             D((16,)), D((16,)), D((16,)), D((16,)), D((17,)), D((17,)), D((1,)), D((1,)), D((NX, NZ)), D((NX, NZ)),
         ],
         compiler_params=pltpu.CompilerParams(

time: 74.4 us -> 73.8 us (level)
  no operation moved by 1% of the time
where the time goes in v4:
time: 73.8 us; the launch traced here: 73.7 us
  Pallas kernels  73 us (99%)
    pallas_call x1, Pallas kernels, on_device(): pl.pallas_call(main_kernel, name='main', out_shape=(shape((2 * HALF, ROWS...  69.4 us
    pallas_call x1, Pallas kernels, on_device(): pl.pallas_call(final_kernel, name='final', out_shape=(shape((voc, WIDTH),...  3.57 us

profile of v4, /device:TPU:1, one launch (start us, length us, event | category | flops | bytes accessed | tf_op | source)
XLA Modules:
  0.0 73.7 jit_solution(3417474389754783130)
XLA Ops:
  0.6 69.4 %main.1 = (bf16[1024,128]{1,0:T(8,128)(2,1)}, bf16[128,1024]{1,0:T(8,128)(2,1)}, bf16[2,2,8,16,128]{4,3,2,1,0:T(8,128)(2,1)}, f32[16,128]{1,0:T(8,128)}) custom-call(bf16[256,1024]{1,0:T(8,128)(2,1)} %hidden_hbm.1, f32[1,1024]{1,0:T(1,128)} %bitcast.3, bf16[988,1024]{1,0:T(8,128)(2,1)} %head_hbm.1, s32[2,64]{1,0:T(2,128)} %pos_hbm.3, s32[2,64]{1,0:T(2,128)} %tgt_hbm.1, ...), custom_call_target="tpu_custom_call" | custom-call | tf_op jit(solution)/shard_map/main/pallas_call | solution.py:535
  70.1 3.6 %final.1 = (bf16[988,1024]{1,0:T(8,128)(2,1)}, bf16[256,1024]{1,0:T(8,128)(2,1)}, f32[8,128]{1,0:T(8,128)}, f32[1,1]{1,0:T(1,128)}) custom-call(bf16[1024,128]{1,0:T(8,128)(2,1)} %get-tuple-element.12.dlt_hbm, bf16[128,1024]{1,0:T(8,128)(2,1)} %get-tuple-element.13.normed_hbm, bf16[2,2,8,16,128]{4,3,2,1,0:T(8,128)(2,1)} %get-tuple-element.14.rg_hbm, ...), custom_call_target="tpu_custom_call" | custom-call | tf_op jit(solution)/shard_map/final/pallas_call | solution.py:576

commit v5 on v4

--- a/solution.py
+++ b/solution.py
@@ -16,7 +16,8 @@
 TOK = 256
 WIDTH = 1024
 MODEL = 8192
-HALF = 512
+PARTS = 2
+PART = 1024 // PARTS
 FAR_FIRST = (4, 3, 5, 2, 6, 1, 7)
 NEAR_FIRST = (1, 7, 2, 6, 3, 5, 4)
 
@@ -86,27 +87,32 @@
 ):
     ctx = lax.axis_index("ctx")
     vy = lax.axis_index("vocab")
-    x = ctx // 16
-    z = (ctx // 2) % NZ
-    k = ctx % 2
+    x = lax.div(ctx, 16)
+    z = lax.rem(lax.div(ctx, 2), NZ)
+    k = lax.rem(ctx, 2)
     voc = head.shape[0]
 
+    xs = [x] + [lax.rem(x + d, NX) for d in range(1, NX)]
+    zs = [z] + [lax.rem(z + d, NZ) for d in range(1, NZ)]
+    ys = [vy] + [lax.rem(vy + d, NY) for d in range(1, NY)]
+    pair_x = x + 1 - 2 * lax.rem(x, 2)
+    x16 = [i * 16 for i in xs]
+    z2k = [i * 2 + k for i in zs]
+
     def at_x(d):
-        return (((x + d) % NX) * 16 + z * 2 + k, vy)
+        return (x16[d] + z2k[0], vy)
 
     def at_z(d):
-        return (x * 16 + ((z + d) % NZ) * 2 + k, vy)
+        return (x16[0] + z2k[d], vy)
 
     def at_y(d):
-        return (ctx, (vy + d) % NY)
-
-    pair_x = x + 1 - 2 * (x % 2)
+        return (ctx, ys[d])
 
     def at_pair(d):
-        return (pair_x * 16 + ((z + d) % NZ) * 2 + k, vy)
+        return (pair_x * 16 + z2k[d], vy)
 
     def at_xz(e, d):
-        return (((x + e) % NX) * 16 + ((z + d) % NZ) * 2 + k, vy)
+        return (x16[e] + z2k[d], vy)
 
     plane = [(e, d) for d in FAR_FIRST + (0,) for e in (2, 1, 3, 0) if (e, d) != (0, 0)]
     other = (x * 16 + z * 2 + (1 - k), vy)
@@ -180,7 +186,7 @@
     cx = {}
 
     def forward_x(d):
-        zz = (z - d + NZ) % NZ
+        zz = zs[(NZ - d) % NZ]
         for e in (2, 1, 3):
             cx[d, e] = start(
                 copy(slots.at[x, k, zz], slots.at[x, k, zz], row_x_s.at[d, e], row_x_r.at[d, e], at_x(e))
@@ -200,7 +206,7 @@
     cc = {}
 
     def forward_core(e):
-        xx = (x - e + NX) % NX
+        xx = xs[(NX - e) % NX]
         cc[e] = start(copy(slots.at[xx, k], slots.at[xx, k], row_c_s.at[e], row_c_r.at[e], other))
 
     forward_core(0)
@@ -247,15 +253,15 @@
     store(0, normed_v, normed_out)
 
     load_head.wait()
-    lives = (HALF, voc - HALF)
-    head_part = (head.at[0:HALF], head.at[HALF:voc])
+    lives = [min(PART, voc - h * PART) for h in range(PARTS)]
+    head_part = [head.at[h * PART : h * PART + lives[h]] for h in range(PARTS)]
     own_group = pl.ds(pl.multiple_of(vy * 16, 16), 16)
-    lp[1, :, HALF - 128 :] = jnp.zeros((ROWS, 128), F32)
+    lp[PARTS - 1, :, PART - 128 :] = jnp.zeros((ROWS, 128), F32)
 
     def group(d):
-        return pl.ds(pl.multiple_of(((vy + d) % NY) * 16, 16), 16)
-
-    ways = ((0, 1, 2, 3, slice(0, HALF // 2)), (1, 7, 6, 5, slice(HALF // 2, HALF)))
+        return pl.ds(pl.multiple_of(ys[d] * 16, 16), 16)
+
+    ways = ((0, 1, 2, 3, slice(0, PART // 2)), (1, 7, 6, 5, slice(PART // 2, PART)))
     c1 = {}
 
     def first_sends(h):
@@ -271,8 +277,8 @@
                 copy(lp.at[h, group(three)], relay.at[h, w], rl_s.at[i + 1], rl_r.at[i + 1], at_y(two))
             )
 
-    first_sends(0)
-    first_sends(1)
+    for h in range(PARTS):
+        first_sends(h)
     cl = {}
 
     def pass_on(h):
@@ -290,14 +296,14 @@
             )
 
     is_target = []
-    for h in range(2):
-        entry = iota((ROWS, HALF), 1) + h * HALF
+    for h in range(PARTS):
+        entry = iota((ROWS, PART), 1) + h * PART
         is_target.append((entry + ctx * voc == tgt_c) & (entry < voc))
 
     def over_vocab(left):
         return sum(
             jnp.dot(left[h][:, : lives[h]], head_part[h][...], preferred_element_type=F32)
-            for h in range(2)
+            for h in range(PARTS)
         )
 
     def split(value, buf):
@@ -311,49 +317,39 @@
     ct.wait_recv()
     txbuf[...] = (tbuf[k].astype(F32) + tcrecv[...].astype(F32)).astype(BF16)
     ct = {
-        d: start(copy(txbuf.at[(x + d) % NX], txrecv.at[x], t_s.at[d], t_r.at[d], at_x(d)))
+        d: start(copy(txbuf.at[xs[d]], txrecv.at[x], t_s.at[d], t_r.at[d], at_x(d)))
         for d in (2, 1, 3)
     }
     txrecv[x] = txbuf[x]
-    pass_on(0)
-    pass_on(1)
-    for d in range(1, NX):
-        ct[d].wait_recv()
-    of_targets = jnp.sum(txrecv[...].astype(F32), axis=0)
-    for j in range(NZ):
-        tzbuf[j] = of_targets[:, j * 128 : (j + 1) * 128].astype(BF16)
-    ct = {
-        d: start(copy(tzbuf.at[(z + d) % NZ], tzrecv.at[z], t_s.at[8 + d], t_r.at[8 + d], at_z(d)))
-        for d in FAR_FIRST
-    }
-    tzrecv[z] = tzbuf[z]
-
+    for h in range(PARTS):
+        pass_on(h)
     to_lane = iota((16, ROWS), 1) == vy * 16 + iota((16, ROWS), 0)
     target16 = rows16(tgt_l, vy * 16).astype(jnp.int32) - ctx * voc
     stat_rows = []
     ce = {}
-    for h in range(2):
+    for h in range(PARTS):
         for w in range(2):
             cl[h, w, 0].wait_recv()
             cl[h, w, 1].wait_recv()
         logits = lp[h, own_group]
         for i in range(4):
             logits = logits + lrecv[h, i]
-        lane = iota((16, HALF), 1)
+        lane = iota((16, PART), 1)
         live = lane < lives[h]
         top = jnp.max(jnp.where(live, logits, -jnp.inf), axis=1, keepdims=True)
         shifted = logits - top
         exps = jnp.where(live, jnp.exp(shifted), 0.0)
-        e_all[h, own_group] = exps.astype(BF16)
+        at_target = live & (lane + h * PART == target16)
+        e_all[h, own_group] = jnp.where(at_target, 0.0, exps).astype(BF16)
         stat = (
             top,
             jnp.sum(exps, axis=1, keepdims=True),
             jnp.sum(exps * shifted, axis=1, keepdims=True),
-            jnp.sum(jnp.where(live & (lane + h * HALF == target16), logits, 0.0), axis=1, keepdims=True),
+            jnp.sum(jnp.where(at_target, logits, 0.0), axis=1, keepdims=True),
         )
         stat_rows += [jnp.sum(jnp.where(to_lane, v, 0.0), axis=0, keepdims=True) for v in stat]
-        if h == 1:
-            st_y[vy] = stack_rows(*stat_rows)
+        if h == PARTS - 1:
+            st_y[vy] = jnp.concatenate([stack_rows(*stat_rows[i : i + 8]) for i in range(0, 4 * PARTS, 8)], axis=0)
             cy = to_line(FAR_FIRST, vy, at_y, st_y, st_s, st_r, 0)
         for d in FAR_FIRST:
             ce[h, d] = start(
@@ -363,20 +359,31 @@
                 )
             )
 
+    for d in range(1, NX):
+        ct[d].wait_recv()
+    of_targets = jnp.sum(txrecv[...].astype(F32), axis=0)
+    for j in range(NZ):
+        tzbuf[j] = of_targets[:, j * 128 : (j + 1) * 128].astype(BF16)
+    ct = {
+        d: start(copy(tzbuf.at[zs[d]], tzrecv.at[z], t_s.at[8 + d], t_r.at[8 + d], at_z(d)))
+        for d in FAR_FIRST
+    }
+    tzrecv[z] = tzbuf[z]
+
     for d in range(1, NY):
         cy[d].wait_recv()
     block = jnp.sum(st_y[...], axis=0)
-    tops = (block[0:1], block[4:5])
-    here = combine([block[0:4], block[4:8]])
+    tops = [block[4 * h : 4 * h + 1] for h in range(PARTS)]
+    here = combine([block[4 * h : 4 * h + 4] for h in range(PARTS)])
     st_c[k] = here
     cst = start(copy(st_c.at[k], st_c.at[k], st_s.at[20], st_r.at[20], other))
 
     u = None
-    scales = columns(jnp.exp(tops[0] - here[0:1]), jnp.exp(tops[1] - here[0:1]))
-    for h in range(2):
+    scales = columns(*(jnp.exp(t - here[0:1]) for t in tops))
+    for h in range(PARTS):
         for d in range(1, NY):
             ce[h, d].wait_recv()
-        left = jnp.where(is_target[h], 0.0, scales[h] * e_all[h].astype(F32)).astype(BF16)
+        left = (scales[h] * e_all[h].astype(F32)).astype(BF16)
         part = jnp.dot(left[:, : lives[h]], head_part[h][...], preferred_element_type=F32)
         u = part if u is None else u + part
     split(u, ubuf)
@@ -393,7 +400,7 @@
     for i in range(NX):
         xbuf[i] = (own_s[i] * ubuf[k, i].astype(F32) + other_s[i] * crecv[i].astype(F32)).astype(BF16)
     cu = {
-        d: start(copy(xbuf.at[(x + d) % NX], xrecv.at[x], u_s.at[d], u_r.at[d], at_x(d)))
+        d: start(copy(xbuf.at[xs[d]], xrecv.at[x], u_s.at[d], u_r.at[d], at_x(d)))
         for d in (2, 1, 3)
     }
     xrecv[x] = xbuf[x]
@@ -415,7 +422,7 @@
     for j in range(NZ):
         zbuf[j] = part[:, j * 128 : (j + 1) * 128].astype(BF16)
     cu = {
-        d: start(copy(zbuf.at[(z + d) % NZ], zrecv.at[z], u_s.at[8 + d], u_r.at[8 + d], at_z(d)))
+        d: start(copy(zbuf.at[zs[d]], zrecv.at[z], u_s.at[8 + d], u_r.at[8 + d], at_z(d)))
         for d in FAR_FIRST
     }
     zrecv[z] = zbuf[z]
@@ -453,7 +460,7 @@
     for i in range(NZ):
         dn = dn + scales[i] * zrecv[i].astype(F32)
     rg = turned * dn - taken
-    xl = x % 2
+    xl = lax.rem(x, 2)
     rgall[xl, k, z] = rg.astype(BF16)
     mine = rgall.at[xl, k, z]
     cg = {}
@@ -462,9 +469,9 @@
     for d in FAR_FIRST + (0,):
         cg[8 + d] = start(copy(mine, mine, g_s.at[8 + d], g_r.at[8 + d], at_pair(d)))
     t_c, *w_c = columns(t_l, *(scaled * jnp.exp(t - log_total) for t in tops))
-    for h in range(2):
+    for h in range(PARTS):
         dl = jnp.where(is_target[h], t_c, w_c[h] * e_all[h].astype(F32))
-        dlt[h * HALF : (h + 1) * HALF] = dl.T.astype(BF16)
+        dlt[h * PART : (h + 1) * PART] = dl.T.astype(BF16)
     store(1, dlt, dlt_out)
     for c in cgg:
         c.wait_recv()
@@ -500,8 +507,8 @@
     for c in loads[:2]:
         c.wait()
     stores = []
-    step = WIDTH // 4
-    for i in range(4):
+    step = WIDTH // 2
+    for i in range(2):
         c = slice(i * step, (i + 1) * step)
         gh[:, c] = jnp.dot(dlt[:voc], normed[:, c], preferred_element_type=F32).astype(BF16)
         stores.append(pltpu.make_async_copy(gh.at[:, c], gh_out.at[:, c], sems.at[8 + i]))
@@ -536,7 +543,7 @@
         main_kernel,
         name="main",
         out_shape=(
-            shape((2 * HALF, ROWS), BF16),
+            shape((PARTS * PART, ROWS), BF16),
             shape((ROWS, WIDTH), BF16),
             shape((2, 2, NZ, 16, 128), BF16),
             shape((16, 128), F32),
@@ -548,13 +555,13 @@
             V((2, SEQ_ROWS), I32), V((2, SEQ_ROWS), I32), S((2,), I32), S((2,), I32),
             V((NX, 2, NZ, 16, WIDTH // 2), BF16),
             V((ROWS, WIDTH), F32),
-            V((2, ROWS, HALF), F32),
-            V((2, 2, 16, HALF), F32),
-            V((2, 2, 16, HALF // 2), F32),
-            V((2, 4, 16, HALF), F32),
-            V((2, ROWS, HALF), BF16),
+            V((PARTS, ROWS, PART), F32),
+            V((PARTS, 2, 16, PART), F32),
+            V((PARTS, 2, 16, PART // 2), F32),
+            V((PARTS, 4, 16, PART), F32),
+            V((PARTS, ROWS, PART), BF16),
             V((NY, 1, 128), F32), V((NZ, 1, 128), F32), V((NX, 1, 128), F32), V((2, 1, 128), F32),
-            V((NY, 8, 128), F32), V((NZ, 8, 128), F32), V((NX, 8, 128), F32), V((2, 8, 128), F32),
+            V((NY, 4 * PARTS, 128), F32), V((NZ, 8, 128), F32), V((NX, 8, 128), F32), V((2, 8, 128), F32),
             V((2, NX, 16, WIDTH), BF16), V((NX, 16, WIDTH), BF16),
             V((NX, 16, WIDTH), BF16), V((NX, 16, WIDTH), BF16),
             V((NZ, 16, 128), BF16), V((NZ, 16, 128), BF16),
@@ -563,11 +570,12 @@
             V((NZ, 16, 128), BF16), V((NZ, 16, 128), BF16),
             V((2, 2, NZ, 16, 128), BF16),
             V((NX, NZ, 8, 128), F32), V((2, 8, 128), F32),
-            V((2 * HALF, ROWS), BF16), V((ROWS, WIDTH), BF16), V((16, 128), F32),
+            V((PARTS * PART, ROWS), BF16), V((ROWS, WIDTH), BF16), V((16, 128), F32),
             D((8,)),
             D((8,)), D((8,)), D((8, 4)), D((8, 4)), D((4,)), D((4,)),
-            D((24,)), D((24,)), D((24,)), D((24,)), D((8,)), D((8,)), D((8,)), D((8,)), D((16,)), D((16,)),
-            D((16,)), D((16,)), D((16,)), D((16,)), D((17,)), D((17,)), D((1,)), D((1,)), D((NX, NZ)), D((NX, NZ)),
+            D((24,)), D((24,)), D((24,)), D((24,)),
+            D((4 * PARTS,)), D((4 * PARTS,)), D((4 * PARTS,)), D((4 * PARTS,)), D((8 * PARTS,)), D((8 * PARTS,)),
+            D((20,)), D((20,)), D((16,)), D((16,)), D((17,)), D((17,)), D((1,)), D((1,)), D((NX, NZ)), D((NX, NZ)),
         ],
         compiler_params=pltpu.CompilerParams(
             collective_id=0, has_side_effects=True, vmem_limit_bytes=60 << 20
@@ -585,7 +593,7 @@
         in_specs=[hbm] * 5,
         out_specs=(hbm, hbm, hbm, sm),
         scratch_shapes=[
-            V((2 * HALF, ROWS), BF16), V((ROWS, WIDTH), BF16), V((2, 2, NZ, 16, 128), BF16),
+            V((PARTS * PART, ROWS), BF16), V((ROWS, WIDTH), BF16), V((2, 2, NZ, 16, 128), BF16),
             V((16, 128), F32), V((2, SEQ_ROWS), I32),
             V((voc, WIDTH), BF16), V((TOK, WIDTH), BF16), D((12,)),
         ],

time: 73.8 us -> 73.8 us (level)
  no operation moved by 1% of the time
where the time goes in v5:
time: 73.8 us; the launch traced here: 73.6 us
  Pallas kernels  73 us (99%)
    pallas_call x1, Pallas kernels, on_device(): pl.pallas_call(main_kernel, name='main', out_shape=(shape((PARTS * PART,...  69.5 us
    pallas_call x1, Pallas kernels, on_device(): pl.pallas_call(final_kernel, name='final', out_shape=(shape((voc, WIDTH),...  3.52 us

profile of v5, /device:TPU:1, one launch (start us, length us, event | category | flops | bytes accessed | tf_op | source)
XLA Modules:
  0.0 73.6 jit_solution(5396936541119489895)
XLA Ops:
  0.6 69.5 %main.1 = (bf16[1024,128]{1,0:T(8,128)(2,1)}, bf16[128,1024]{1,0:T(8,128)(2,1)}, bf16[2,2,8,16,128]{4,3,2,1,0:T(8,128)(2,1)}, f32[16,128]{1,0:T(8,128)}) custom-call(bf16[256,1024]{1,0:T(8,128)(2,1)} %hidden_hbm.1, f32[1,1024]{1,0:T(1,128)} %bitcast.3, bf16[988,1024]{1,0:T(8,128)(2,1)} %head_hbm.1, s32[2,64]{1,0:T(2,128)} %pos_hbm.3, s32[2,64]{1,0:T(2,128)} %tgt_hbm.1, ...), custom_call_target="tpu_custom_call" | custom-call | tf_op jit(solution)/shard_map/main/pallas_call | solution.py:542
  70.1 3.5 %final.1 = (bf16[988,1024]{1,0:T(8,128)(2,1)}, bf16[256,1024]{1,0:T(8,128)(2,1)}, f32[8,128]{1,0:T(8,128)}, f32[1,1]{1,0:T(1,128)}) custom-call(bf16[1024,128]{1,0:T(8,128)(2,1)} %get-tuple-element.12.dlt_hbm, bf16[128,1024]{1,0:T(8,128)(2,1)} %get-tuple-element.13.normed_hbm, bf16[2,2,8,16,128]{4,3,2,1,0:T(8,128)(2,1)} %get-tuple-element.14.rg_hbm, ...), custom_call_target="tpu_custom_call" | custom-call | tf_op jit(solution)/shard_map/final/pallas_call | solution.py:584
